TPU v7x, 512 devices: a whole 4x4x16 slice. The times are simulated.
512 devices in a mesh: row: 32 (over z, core), col: 16 (over y, x).
Axes of the slice: x: 4, y: 4, z: 16, core: 2. Of those that a mesh axis runs over, the one named last changes fastest.
Arguments:
- slab: float32 [65536, 4096], P('row', 'col'), may hold values from -6 to 6
- panel: float32 [65536, 128], P(('row', 'col')), may hold values from -0.03125 to 0.03125
- tfactor: float32 [128, 128], replicated, as said below
- other_av: float32 [65536, 128], P(('row', 'col')), may hold values from -6 to 6
Outputs:
- updated: float32 [65536, 4096], P('row', 'col')
- correction: float32 [65536, 128], P(('row', 'col'))
Inputs may be any that keep to these rules, and one draw needn't show every extreme that they name: `tfactor`: upper triangular.
All inputs are finite; a program needn't handle non-finite values.
Results may differ from a plain program's by a relative error of at most 0.00007.
Values sent between devices are 32-bit elements; how exact they have to be, the bound alone decides.
No kernel may reach another device: no remote copies, remote signals or barrier semaphores. Data moves between devices by JAX's collectives and lax.ppermute only.
A program may use at most 64 MiB of HBM per device.

v0:
```python
import jax
import jax.numpy as jnp
from jax import lax
from jax.sharding import PartitionSpec as P


def from_root(value, axis, source):
    kept = jnp.where(lax.axis_index(axis) == source, value, 0).astype(value.dtype)
    return lax.psum(kept, axis)


def on_device(slab, panel, tfactor, other_av):
    high = lax.Precision.HIGHEST
    rows = slab.shape[0]
    width = slab.shape[1]
    nrow = lax.axis_size("row")
    ncol = lax.axis_size("col")
    block = rows // ncol
    col_index = lax.axis_index("col")
    start = rows * nrow // 2 + col_index * width
    root = start // rows
    offset = start - root * rows
    panel_rows = lax.all_gather(panel, "col", axis=0, tiled=True)
    piece = lax.dynamic_slice_in_dim(panel_rows, offset, width, 0)
    slab_panel = from_root(piece, "row", root)
    local_term = jnp.dot(slab, slab_panel, precision=high, preferred_element_type=jnp.float32)
    segment = lax.dynamic_slice_in_dim(local_term, col_index * block, block, 0) + other_av
    local_term = lax.dynamic_update_slice_in_dim(local_term, segment, col_index * block, 0)
    product_full = lax.psum(local_term, "col")
    wmat_full = jnp.dot(product_full, tfactor, precision=high, preferred_element_type=jnp.float32)
    inner_part = jnp.dot(
        panel_rows.T, wmat_full, precision=high, preferred_element_type=jnp.float32
    )
    inner = lax.psum(inner_part, "row")
    shifted = jnp.dot(tfactor.T, inner, precision=high, preferred_element_type=jnp.float32)
    correction_full = wmat_full - 0.5 * jnp.dot(
        panel_rows, shifted, precision=high, preferred_element_type=jnp.float32
    )
    correction = lax.dynamic_slice_in_dim(correction_full, col_index * block, block, 0)
    corr_piece = lax.dynamic_slice_in_dim(correction_full, offset, width, 0)
    slab_correction = from_root(corr_piece, "row", root)
    updated = slab - jnp.dot(
        panel_rows, slab_correction.T, precision=high, preferred_element_type=jnp.float32
    )
    updated = updated - jnp.dot(
        correction_full, slab_panel.T, precision=high, preferred_element_type=jnp.float32
    )
    return (updated, correction)


def solution(mesh):
    placed = (P("row", "col"), P(("row", "col"), None), P(), P(("row", "col"), None))
    return jax.shard_map(
        on_device,
        mesh=mesh,
        in_specs=placed,
        out_specs=(P("row", "col"), P(("row", "col"), None)),
        check_vma=False,
    )
```

profile of v0, /device:TPU:1, one launch (start us, length us, event | category | flops | bytes accessed | tf_op | source)
XLA Modules:
  0.0 787.2 jit_solution(1186248330590596701)
XLA Ops:
  7.2 0.0 copy-start
  7.2 0.0 all-gather.2.cloned.1.call-start
  7.2 0.7 all-gather.2.cloned.1.call-update
  7.9 0.0 all-reduce.5.cloned.1.call-start
  8.0 65.0 %all-gather.2.cloned.1.call-done = f32[2048,128]{1,0:T(8,128)} async-done(((f32[128,128]{1,0:T(8,128)}), f32[2048,128]{1,0:T(8,128)}) %all-gather.2.cloned.1.call-update) | async-done | bytes 1048592 | tf_op jit(solution)/shard_map/all_gather | solution.py:23
  73.0 1.6 dynamic-slice_select_fusion.1
  74.5 0.0 all-reduce.5.cloned.1.call-update
  74.5 0.0 all-reduce.7.cloned.1.call-start
  74.6 0.9 copy.6
  75.5 196.9 %all-reduce.5.cloned.1.call-done = f32[256,128]{1,0:T(8,128)} async-done(((f32[256,128]{1,0:T(8,128)}), f32[256,128]{1,0:T(8,128)}) %all-reduce.5.cloned.1.call-update) | async-done | bytes 131088 | tf_op jit(solution)/shard_map/psum | solution.py:9
  272.5 4.0 fusion.5
  276.5 0.1 copy.14
  276.6 1.0 copy-done.4
  277.6 0.0 all-reduce.7.cloned.1.call-update
  277.6 0.0 all-reduce.9.cloned.1.call-start
  277.7 112.2 %all-reduce.7.cloned.1.call-done = f32[2048,128]{0,1:T(8,128)} async-done(((f32[2048,128]{0,1:T(8,128)}), f32[2048,128]{0,1:T(8,128)}) %all-reduce.7.cloned.1.call-update) | async-done | bytes 1048592 | tf_op jit(solution)/shard_map/psum | solution.py:29
  389.8 3.0 fusion.6
  392.9 2.4 convolution_bitcast_fusion.1
  395.3 0.0 all-reduce.9.cloned.1.call-update
  395.3 0.0 all-reduce.11.cloned.1.call-start
  395.4 2.9 copy.8
  398.3 181.8 %all-reduce.9.cloned.1.call-done = f32[128,128]{0,1:T(8,128)} async-done(((f32[128,128]{0,1:T(8,128)}), f32[128,128]{0,1:T(8,128)}) %all-reduce.9.cloned.1.call-update) | async-done | bytes 65552 | tf_op jit(solution)/shard_map/psum | solution.py:34
  580.1 1.0 fusion.7
  581.1 1.0 fusion.3
  582.1 1.0 copy-done.3
  583.1 0.6 dynamic-slice_select_fusion
  583.8 0.0 all-reduce.11.cloned.1.call-update
  583.8 4.4 fusion.8
  588.1 1.5 constant_dynamic-slice_fusion
  589.6 183.3 %all-reduce.11.cloned.1.call-done = f32[256,128]{1,0:T(8,128)} async-done(((f32[256,128]{1,0:T(8,128)}), f32[256,128]{1,0:T(8,128)}) %all-reduce.11.cloned.1.call-update) | async-done | bytes 131088 | tf_op jit(solution)/shard_map/psum | solution.py:9
  772.9 4.9 fusion.1
  777.8 2.9 copy.10
  (10 shorter events, 0.0 us)
Async XLA Ops:
  7.2 382.6 %copy-start = (f32[128,128]{1,0:T(8,128)S(1)}, f32[128,128]{1,0:T(8,128)}, u32[]{:S(2)}) copy-start(f32[128,128]{1,0:T(8,128)} %param.6) | copy-start | bytes 196612
  7.2 65.8 %all-gather.2.cloned.1.call-start = ((), (), s32[]{:S(2)}) async-start(), calls=%async_computation | async-start | bytes 1114112 | tf_op jit(solution)/shard_map/all_gather | solution.py:23
  7.9 264.6 %all-reduce.5.cloned.1.call-start = ((), (), s32[]{:S(2)}) async-start(), calls=%async_computation.1 | async-start | bytes 262144 | tf_op jit(solution)/shard_map/psum | solution.py:9
  74.5 315.3 %all-reduce.7.cloned.1.call-start = ((), (), s32[]{:S(2)}) async-start(), calls=%async_computation.2 | async-start | bytes 2097152 | tf_op jit(solution)/shard_map/psum | solution.py:29
  276.6 116.3 %copy-start.1 = (f32[2048,128]{1,0:T(8,128)S(1)}, f32[2048,128]{1,0:T(8,128)}, u32[]{:S(2)}) copy-start(f32[2048,128]{1,0:T(8,128)} %all-gather.2.cloned.1.call-done) | copy-start | bytes 3145732
  276.6 1.0 copy-start.4
  277.6 302.5 %all-reduce.9.cloned.1.call-start = ((), (), s32[]{:S(2)}) async-start(), calls=%async_computation.3 | async-start | bytes 131072 | tf_op jit(solution)/shard_map/psum | solution.py:34
  395.3 377.6 %all-reduce.11.cloned.1.call-start = ((), (), s32[]{:S(2)}) async-start(), calls=%async_computation.4 | async-start | bytes 262144 | tf_op jit(solution)/shard_map/psum | solution.py:9
  398.3 185.5 %copy-start.5 = (f32[256,128]{1,0:T(8,128)S(1)}, f32[256,128]{1,0:T(8,128)}, u32[]{:S(2)}) copy-start(f32[256,128]{1,0:T(8,128)} %all-reduce.5.cloned.1.call-done) | copy-start | bytes 393220
  582.1 1.0 copy-start.3
  583.1 189.8 %copy-start.2 = (f32[2048,256]{0,1:T(8,128)S(1)}, f32[2048,256]{0,1:T(8,128)}, u32[]{:S(2)}) copy-start(f32[2048,256]{0,1:T(8,128)} %copy.8) | copy-start | bytes 6291460
Sparse Core Ops, SparseCore 0:
  11.0 61.8 all-gather.1
  75.8 196.5 all-reduce.4
  277.7 112.0 all-reduce.6
  395.4 184.5 all-reduce.8
  583.9 188.9 all-reduce.10
where the time goes:
time: 788 us; the launch traced here: 787 us
  waiting for transfers between devices  740 us (94%)
  matrix products  20.8 us (3%)
  between operations  13.9 us (2%)
  local copies, waits for them, and re-layouts  10.3 us (1%)
    psum x2, waiting for transfers between devices, from_root(): return lax.psum(kept, axis)  380 us
    psum x1, waiting for transfers between devices, on_device(): inner = lax.psum(inner_part, 'row')  182 us
    psum x1, waiting for transfers between devices, on_device(): product_full = lax.psum(local_term, 'col')  112 us
    all_gather x1, waiting for transfers between devices, on_device(): panel_rows = lax.all_gather(panel, 'col', axis=0, tiled=True)  65 us
  transfers between devices with their start and end apart: 5, of which 5 were waited for; matrix products, arithmetic and copies ran while one was open for 1% of the time, Pallas kernels for 0%

commit v1 on v0

v1 whole, which is shorter than its diff:
```python
import jax
import jax.numpy as jnp
from jax import lax
from jax.sharding import Mesh, PartitionSpec as P

ROW = ("z", "core")
COL = ("y", "x")
ALL = ROW + COL


def dot(a, b, dims=((1,), (0,))):
    return lax.dot_general(
        a, b, (dims, ((), ())), precision=lax.Precision.HIGHEST, preferred_element_type=jnp.float32
    )


def to_all(value, axis):
    spread = jnp.broadcast_to(value, (lax.axis_size(axis),) + value.shape)
    return lax.all_to_all(spread, axis, 0, 0)


def slab_rows(value):
    nz, ncore, ncol = lax.axis_size("z"), lax.axis_size("core"), lax.axis_size(COL)
    root = nz // 2

    def index(z, core, col):
        return (z * ncore + core) * ncol + col

    held = 0
    for target in (0, nz // 4, nz // 2, 3 * nz // 4):
        pairs = [
            (index(root, k, c), index(target, c % 2, (k * ncol + c) // 2))
            for k in range(ncore)
            for c in range(ncol)
        ]
        held = held + lax.ppermute(value, ALL, pairs)
    step = nz // 8
    while step:
        held = held + lax.ppermute(held, "z", [(z, z + step) for z in range(0, nz, 2 * step)])
        step //= 2
    other = lax.ppermute(held, "core", [(0, 1), (1, 0)])
    first = lax.axis_index("core") == 0
    return jnp.concatenate([jnp.where(first, held, other), jnp.where(first, other, held)], axis=0)


def on_device(slab, panel, tfactor, other_av):
    ncol = lax.axis_size(COL)
    block = panel.shape[0]
    panel_rows = to_all(panel, COL).reshape(ncol * block, -1)
    slab_panel = slab_rows(panel)
    term = dot(slab, slab_panel)
    cross = dot(panel_rows, term, ((0,), (0,))) + dot(panel, other_av, ((0,), (0,)))
    sent = jnp.concatenate(
        [term.reshape(ncol, block, -1), cross.reshape(ncol, block // ncol, -1)], axis=1
    )
    summed = lax.all_to_all(sent, COL, 0, 0).sum(axis=0)
    wmat = dot(summed[:block] + other_av, tfactor)
    wmat_rows = to_all(wmat, COL).reshape(ncol * block, -1)
    slab_wmat = slab_rows(wmat)
    part = summed[block:]
    part = part + lax.ppermute(part, "core", [(0, 1), (1, 0)])
    part = to_all(part, "z").sum(axis=0)
    cross = to_all(part, COL).reshape(block, -1)
    middle = dot(dot(tfactor, cross, ((0,), (0,))), tfactor)
    correction = wmat - 0.5 * dot(panel, middle)
    left = jnp.concatenate([panel_rows, wmat_rows], axis=1)
    right = jnp.concatenate([slab_wmat - 0.5 * dot(slab_panel, middle + middle.T), slab_panel], axis=1)
    updated = slab - dot(left, right, ((1,), (1,)))
    return updated, correction


def solution(mesh):
    nrow, ncol = mesh.devices.shape
    grid = Mesh(mesh.devices.reshape(nrow // 2, 2, 4, ncol // 4), ALL)
    placed = (P(ROW, COL), P(ALL, None), P(), P(ALL, None))
    return jax.shard_map(
        on_device,
        mesh=grid,
        in_specs=placed,
        out_specs=(P(ROW, COL), P(ALL, None)),
        check_vma=False,
    )
```

time: 788 us -> 148 us (0.19)
  the two profiles are of different devices: /device:TPU:1 before, /device:TPU:96 now
where the time goes in v1:
time: 148 us; the launch traced here: 147 us
  waiting for transfers between devices  60.3 us (41%)
  starting transfers between devices  51.9 us (35%)
  matrix products  13.2 us (9%)
  blocking collectives  11.8 us (8%)
  local copies, waits for them, and re-layouts  5.06 us (3%)
  other arithmetic  3.41 us (2%)
    ppermute x4, waiting for transfers between devices, slab_rows(): lax.ppermute(held, 'z', [(z, z + step) for z in range(0, nz, 2 * step)])  27.4 us
    all_to_all x3, starting transfers between devices, to_all(): return lax.all_to_all(spread, axis, 0, 0)  23.9 us
    all_to_all x1, waiting for transfers between devices, on_device(): summed = lax.all_to_all(sent, COL, 0, 0).sum(axis=0)  18.6 us
    dot_general x9, matrix products, dot(): lax.dot_general(a, b, (dims, ((), ())), precision=lax.Precision.HIGHEST,...  13.2 us
    all_to_all x3, waiting for transfers between devices, to_all(): return lax.all_to_all(spread, axis, 0, 0)  12.2 us
    all_to_all x1, blocking collectives, to_all(): return lax.all_to_all(spread, axis, 0, 0)  11.8 us
    all_to_all x1, starting transfers between devices, on_device(): summed = lax.all_to_all(sent, COL, 0, 0).sum(axis=0)  9.99 us
    ppermute x2, starting transfers between devices, slab_rows(): other = lax.ppermute(held, 'core', [(0, 1), (1, 0)])  6.76 us
  transfers between devices with their start and end apart: 19, of which 6 were waited for; matrix products, arithmetic and copies ran while one was open for 9% of the time, Pallas kernels for 0%

profile of v1, /device:TPU:96, one launch (start us, length us, event | category | flops | bytes accessed | tf_op | source)
XLA Modules:
  0.0 146.8 jit_solution(1716487096392980118)
XLA Ops:
  0.6 0.8 collective-permute-start.3
  1.4 0.7 collective-permute-start.2
  2.1 0.7 collective-permute-start.1
  2.8 0.7 collective-permute-start
  3.5 1.9 %broadcast_in_dim.12 = f32[16,128,128]{2,1,0:T(8,128)} broadcast(f32[128,128]{1,0:T(8,128)} %param.5), dimensions={1,2} | broadcast | bytes 1114112 | tf_op jit(solution)/shard_map/broadcast_in_dim | solution.py:18
  5.4 7.0 %all-to-all-start = ((f32[16,128,128]{2,1,0:T(8,128)}), f32[16,128,128]{2,1,0:T(8,128)S(1)}, u32[]{:S(2)}, u32[]{:S(2)}) async-start(f32[16,128,128]{2,1,0:T(8,128)} %broadcast_in_dim.12), calls=%async_computation | async-start | bytes 2097152 | tf_op jit(solution)/shard_map/all_to_all | solution.py:19
  12.5 0.7 collective-permute-start.4
  13.2 1.3 collective-permute-start.5
  14.5 17.8 %collective-permute-done.5 = f32[128,128]{1,0:T(8,128)S(1)} collective-permute-done((f32[128,128]{1,0:T(8,128)S(1)}, f32[128,128]{1,0:T(8,128)S(1)}, u32[]{:S(2)}, u32[]{:S(2)}) %collective-permute-start.5) | collective-permute-done | bytes 65568 | tf_op jit(solution)/shard_map/ppermute | solution.py:39
  32.3 4.9 %collective-permute-start.6 = (f32[128,128]{1,0:T(8,128)S(1)}, f32[128,128]{1,0:T(8,128)S(1)}, u32[]{:S(2)}, u32[]{:S(2)}) collective-permute-start(f32[128,128]{1,0:T(8,128)S(1)} %add.46), channel_id=1, source_target_pairs={{0,16},{16,0},{1,17},{17,1},{2,18},{18,2},{3,19},{19,3},{4,20},{20... | collective-permute-start | bytes 196616 | tf_op jit(solution)/shard_map/ppermute | solution.py:41
  37.1 0.9 collective-permute-done.6
  38.0 3.9 %fusion.11 = f32[128,2048]{1,0:T(8,128)S(1)} fusion(f32[2048,256]{1,0:T(8,128)} %param.4, f32[128,128]{1,0:T(8,128)S(1)} %get-tuple-element.5, f32[128,128]{1,0:T(8,128)S(1)} %get-tuple-element.4), kind=kOutput, calls=%fused_computation.19 | convolution fusion | flops 805339136 | bytes 3276800 | tf_op jit(solution)/shard_map/dot_general | solution.py:12
  42.3 1.8 %convolution_bitcast_fusion = f32[128,128]{1,0:T(8,128)S(1)} fusion(f32[128,2048]{1,0:T(8,128)S(1)} %fusion.11, f32[2048,128]{1,0:T(8,128)S(1)} %bitcast.29), kind=kOutput, calls=%fused_computation.10 | convolution fusion | flops 402653184 | bytes 2162688 | tf_op jit(solution)/shard_map/dot_general | solution.py:12
  44.4 1.1 pad_maximum_fusion
  45.5 10.0 %all-to-all-start.1 = ((f32[16,136,128]{2,1,0:T(8,128)}), f32[16,136,128]{2,1,0:T(8,128)S(1)}, u32[]{:S(2)}, u32[]{:S(2)}) async-start(f32[16,136,128]{2,1,0:T(8,128)} %pad_maximum_fusion), calls=%async_computation.1 | async-start | bytes 2228224 | tf_op jit(solution)/shard_map/all_to_all | solution.py:56
  55.6 18.6 %all-to-all-done.1 = f32[16,136,128]{2,1,0:T(8,128)S(1)} async-done(((f32[16,136,128]{2,1,0:T(8,128)}), f32[16,136,128]{2,1,0:T(8,128)S(1)}, u32[]{:S(2)}, u32[]{:S(2)}) %all-to-all-start.1) | async-done | bytes 1114144 | tf_op jit(solution)/shard_map/all_to_all | solution.py:56
  74.7 0.7 collective-permute-start.10
  77.5 1.9 %collective-permute-start.14 = (f32[8,128]{0,1:T(8,128)S(1)}, f32[8,128]{0,1:T(8,128)S(1)}, u32[]{:S(2)}, u32[]{:S(2)}) collective-permute-start(f32[8,128]{0,1:T(8,128)S(1)} %copy.27), channel_id=1, source_target_pairs={{0,16},{16,0},{1,17},{17,1},{2,18},{18,2},{3,19},{19,3},{4,20},{20... | collective-permute-start | bytes 12296 | tf_op jit(solution)/shard_map/ppermute | solution.py:61
  79.4 1.2 collective-permute-done.14
  81.3 12.4 %all-to-all-start.3 = ((f32[16,8,128]{2,1,0:T(8,128)}), f32[16,8,128]{2,1,0:T(8,128)S(1)}, u32[]{:S(2)}, u32[]{:S(2)}) async-start(f32[16,8,128]{2,1,0:T(8,128)} %broadcast_in_dim.14), calls=%async_computation.3 | async-start | bytes 131072 | tf_op jit(solution)/shard_map/all_to_all | solution.py:19
  94.5 1.3 collective-permute-start.12
  95.8 9.6 %collective-permute-done.12 = f32[128,128]{1,0:T(8,128)S(1)} collective-permute-done((f32[128,128]{1,0:T(8,128)S(1)}, f32[128,128]{1,0:T(8,128)S(1)}, u32[]{:S(2)}, u32[]{:S(2)}) %collective-permute-start.12) | collective-permute-done | bytes 65568 | tf_op jit(solution)/shard_map/ppermute | solution.py:39
  106.1 1.9 %collective-permute-start.13 = (f32[128,128]{1,0:T(8,128)}, f32[128,128]{1,0:T(8,128)}, u32[]{:S(2)}, u32[]{:S(2)}) collective-permute-start(f32[128,128]{1,0:T(8,128)} %add.53), channel_id=1, source_target_pairs={{0,16},{16,0},{1,17},{17,1},{2,18},{18,2},{3,19},{19,3},{4,20},{20... | collective-permute-start | bytes 196616 | tf_op jit(solution)/shard_map/ppermute | solution.py:41
  108.0 11.8 %all_to_all.25 = f32[16,8,128]{2,1,0:T(8,128)S(1)} all-to-all(f32[16,8,128]{2,1,0:T(8,128)S(1)} %broadcast_in_dim.15), channel_id=1, replica_groups=mesh['z'=16,'core'=2,'y'=4,'x'=4] {'y','x'}, dimensions={0} | all-to-all | bytes 131072 | tf_op jit(solution)/shard_map/all_to_all | solution.py:19
  119.8 1.1 broadcast_in_dim.13
  120.9 4.5 %all-to-all-start.2 = ((f32[16,128,128]{2,1,0:T(8,128)}), f32[16,128,128]{2,1,0:T(8,128)}, u32[]{:S(2)}, u32[]{:S(2)}) async-start(f32[16,128,128]{2,1,0:T(8,128)} %broadcast_in_dim.13), calls=%async_computation.2 | async-start | bytes 2097152 | tf_op jit(solution)/shard_map/all_to_all | solution.py:19
  125.4 1.5 %broadcast_select_fusion.1 = (f32[128,128]{1,0:T(8,128)}, f32[128,128]{1,0:T(8,128)}) fusion(f32[128,128]{1,0:T(8,128)} %add.53, f32[128,128]{1,0:T(8,128)} %collective-permute-done.13, pred[]{:T(512)S(6)} %eq.4), kind=kLoop, calls=%fused_computation.28 | loop fusion | flops 32768 | bytes 262145 | tf_op jit(solution)/shard_map/jit(_where)/select_n | solution.py:43
  127.5 0.7 copy.19
  128.2 0.8 fusion.4
  129.0 1.2 maximum_subtract_fusion
  130.2 12.2 %all-to-all-done.2 = f32[16,128,128]{2,1,0:T(8,128)} async-done(((f32[16,128,128]{2,1,0:T(8,128)}), f32[16,128,128]{2,1,0:T(8,128)}, u32[]{:S(2)}, u32[]{:S(2)}) %all-to-all-start.2) | async-done | bytes 1048608 | tf_op jit(solution)/shard_map/all_to_all | solution.py:19
  142.4 4.4 %convolution_subtract_fusion = f32[2048,256]{1,0:T(8,128)} fusion(f32[2048,256]{1,0:T(8,128)S(1)} %copy-done.1, f32[2048,128]{1,0:T(8,128)} %bitcast.5, f32[2048,128]{1,0:T(8,128)S(1)} %bitcast.30, f32[128,128]{1,0:T(8,128)S(1)} %get-tuple-element.5, f32[128,128]{1,0:T(8,128)S(1)} %get-tuple-element.4, f32[256,128]{1,0:T(8,128)S(1)} %maximum_subtract_fusion), kind=kOutput, calls=%fused_computation | convolution fusion | flops 1611792384 | bytes 6553600 | tf_op jit(solution)/shard_map/dot_general | solution.py:12
  (48 shorter events, 6.0 us)
Async XLA Ops:
  0.6 73.7 %copy-start = (f32[128,128]{1,0:T(8,128)S(1)}, f32[128,128]{1,0:T(8,128)}, u32[]{:S(2)}) copy-start(f32[128,128]{1,0:T(8,128)} %param.6) | copy-start | bytes 196612
  0.6 11.8 %collective-permute-start.3 = (f32[128,128]{1,0:T(8,128)}, f32[128,128]{1,0:T(8,128)S(1)}, u32[]{:S(2)}, u32[]{:S(2)}) collective-permute-start(f32[128,128]{1,0:T(8,128)} %param.5), channel_id=1, source_target_pairs={{256,384},{257,400},{258,385},{259,401},{260,386},{261,402},{262,3... | collective-permute-start | bytes 196616 | tf_op jit(solution)/shard_map/ppermute | solution.py:36
  1.4 11.0 %collective-permute-start.2 = (f32[128,128]{1,0:T(8,128)}, f32[128,128]{1,0:T(8,128)S(1)}, u32[]{:S(2)}, u32[]{:S(2)}) collective-permute-start(f32[128,128]{1,0:T(8,128)} %param.5), channel_id=1, source_target_pairs={{256,256},{257,272},{258,257},{259,273},{260,258},{261,274},{262,2... | collective-permute-start | bytes 196616 | tf_op jit(solution)/shard_map/ppermute | solution.py:36
  2.1 10.3 %collective-permute-start.1 = (f32[128,128]{1,0:T(8,128)}, f32[128,128]{1,0:T(8,128)S(1)}, u32[]{:S(2)}, u32[]{:S(2)}) collective-permute-start(f32[128,128]{1,0:T(8,128)} %param.5), channel_id=1, source_target_pairs={{256,128},{257,144},{258,129},{259,145},{260,130},{261,146},{262,1... | collective-permute-start | bytes 196616 | tf_op jit(solution)/shard_map/ppermute | solution.py:36
  2.8 9.7 %collective-permute-start = (f32[128,128]{1,0:T(8,128)}, f32[128,128]{1,0:T(8,128)S(1)}, u32[]{:S(2)}, u32[]{:S(2)}) collective-permute-start(f32[128,128]{1,0:T(8,128)} %param.5), channel_id=1, source_target_pairs={{256,0},{257,16},{258,1},{259,17},{260,2},{261,18},{262,3},{263,19... | collective-permute-start | bytes 196616 | tf_op jit(solution)/shard_map/ppermute | solution.py:36
  5.4 36.9 %all-to-all-start = ((f32[16,128,128]{2,1,0:T(8,128)}), f32[16,128,128]{2,1,0:T(8,128)S(1)}, u32[]{:S(2)}, u32[]{:S(2)}) async-start(f32[16,128,128]{2,1,0:T(8,128)} %broadcast_in_dim.12), calls=%async_computation | async-start | bytes 2097152 | tf_op jit(solution)/shard_map/all_to_all | solution.py:19
  12.5 0.7 collective-permute-start.4
  13.2 19.1 %collective-permute-start.5 = (f32[128,128]{1,0:T(8,128)S(1)}, f32[128,128]{1,0:T(8,128)S(1)}, u32[]{:S(2)}, u32[]{:S(2)}) collective-permute-start(f32[128,128]{1,0:T(8,128)S(1)} %add.45), channel_id=1, source_target_pairs={{0,32},{64,96},{128,160},{192,224},{256,288},{320,352},{384,416},{... | collective-permute-start | bytes 196616 | tf_op jit(solution)/shard_map/ppermute | solution.py:39
  32.3 5.7 %collective-permute-start.6 = (f32[128,128]{1,0:T(8,128)S(1)}, f32[128,128]{1,0:T(8,128)S(1)}, u32[]{:S(2)}, u32[]{:S(2)}) collective-permute-start(f32[128,128]{1,0:T(8,128)S(1)} %add.46), channel_id=1, source_target_pairs={{0,16},{16,0},{1,17},{17,1},{2,18},{18,2},{3,19},{19,3},{4,20},{20... | collective-permute-start | bytes 196616 | tf_op jit(solution)/shard_map/ppermute | solution.py:41
  41.9 2.2 %copy-start.2 = (f32[128,128]{1,0:T(8,128)S(1)}, f32[128,128]{1,0:T(8,128)}, u32[]{:S(2)}) copy-start(f32[128,128]{1,0:T(8,128)} %param.5) | copy-start | bytes 196612
  41.9 2.2 %copy-start.3 = (f32[128,128]{1,0:T(8,128)S(1)}, f32[128,128]{1,0:T(8,128)}, u32[]{:S(2)}) copy-start(f32[128,128]{1,0:T(8,128)} %param.7) | copy-start | bytes 196612
  45.5 28.7 %all-to-all-start.1 = ((f32[16,136,128]{2,1,0:T(8,128)}), f32[16,136,128]{2,1,0:T(8,128)S(1)}, u32[]{:S(2)}, u32[]{:S(2)}) async-start(f32[16,136,128]{2,1,0:T(8,128)} %pad_maximum_fusion), calls=%async_computation.1 | async-start | bytes 2228224 | tf_op jit(solution)/shard_map/all_to_all | solution.py:56
  74.7 19.0 %collective-permute-start.10 = (f32[128,128]{1,0:T(8,128)S(1)}, f32[128,128]{1,0:T(8,128)S(1)}, u32[]{:S(2)}, u32[]{:S(2)}) collective-permute-start(f32[128,128]{1,0:T(8,128)S(1)} %fusion.14), channel_id=1, source_target_pairs={{256,384},{257,400},{258,385},{259,401},{260,386},{261,402},{262,3... | collective-permute-start | bytes 196616 | tf_op jit(solution)/shard_map/ppermute | solution.py:36
  75.3 18.4 %collective-permute-start.9 = (f32[128,128]{1,0:T(8,128)S(1)}, f32[128,128]{1,0:T(8,128)S(1)}, u32[]{:S(2)}, u32[]{:S(2)}) collective-permute-start(f32[128,128]{1,0:T(8,128)S(1)} %fusion.14), channel_id=1, source_target_pairs={{256,256},{257,272},{258,257},{259,273},{260,258},{261,274},{262,2... | collective-permute-start | bytes 196616 | tf_op jit(solution)/shard_map/ppermute | solution.py:36
  76.0 17.7 %collective-permute-start.8 = (f32[128,128]{1,0:T(8,128)S(1)}, f32[128,128]{1,0:T(8,128)S(1)}, u32[]{:S(2)}, u32[]{:S(2)}) collective-permute-start(f32[128,128]{1,0:T(8,128)S(1)} %fusion.14), channel_id=1, source_target_pairs={{256,128},{257,144},{258,129},{259,145},{260,130},{261,146},{262,1... | collective-permute-start | bytes 196616 | tf_op jit(solution)/shard_map/ppermute | solution.py:36
  76.7 17.1 %collective-permute-start.7 = (f32[128,128]{1,0:T(8,128)S(1)}, f32[128,128]{1,0:T(8,128)S(1)}, u32[]{:S(2)}, u32[]{:S(2)}) collective-permute-start(f32[128,128]{1,0:T(8,128)S(1)} %fusion.14), channel_id=1, source_target_pairs={{256,0},{257,16},{258,1},{259,17},{260,2},{261,18},{262,3},{263,19... | collective-permute-start | bytes 196616 | tf_op jit(solution)/shard_map/ppermute | solution.py:36
  77.5 3.1 %collective-permute-start.14 = (f32[8,128]{0,1:T(8,128)S(1)}, f32[8,128]{0,1:T(8,128)S(1)}, u32[]{:S(2)}, u32[]{:S(2)}) collective-permute-start(f32[8,128]{0,1:T(8,128)S(1)} %copy.27), channel_id=1, source_target_pairs={{0,16},{16,0},{1,17},{17,1},{2,18},{18,2},{3,19},{19,3},{4,20},{20... | collective-permute-start | bytes 12296 | tf_op jit(solution)/shard_map/ppermute | solution.py:61
  81.3 26.6 %all-to-all-start.3 = ((f32[16,8,128]{2,1,0:T(8,128)}), f32[16,8,128]{2,1,0:T(8,128)S(1)}, u32[]{:S(2)}, u32[]{:S(2)}) async-start(f32[16,8,128]{2,1,0:T(8,128)} %broadcast_in_dim.14), calls=%async_computation.3 | async-start | bytes 131072 | tf_op jit(solution)/shard_map/all_to_all | solution.py:19
  93.8 0.7 collective-permute-start.11
  94.5 10.9 %collective-permute-start.12 = (f32[128,128]{1,0:T(8,128)S(1)}, f32[128,128]{1,0:T(8,128)S(1)}, u32[]{:S(2)}, u32[]{:S(2)}) collective-permute-start(f32[128,128]{1,0:T(8,128)S(1)} %add.52), channel_id=1, source_target_pairs={{0,32},{64,96},{128,160},{192,224},{256,288},{320,352},{384,416},{... | collective-permute-start | bytes 196616 | tf_op jit(solution)/shard_map/ppermute | solution.py:39
  106.1 19.3 %collective-permute-start.13 = (f32[128,128]{1,0:T(8,128)}, f32[128,128]{1,0:T(8,128)}, u32[]{:S(2)}, u32[]{:S(2)}) collective-permute-start(f32[128,128]{1,0:T(8,128)} %add.53), channel_id=1, source_target_pairs={{0,16},{16,0},{1,17},{17,1},{2,18},{18,2},{3,19},{19,3},{4,20},{20... | collective-permute-start | bytes 196616 | tf_op jit(solution)/shard_map/ppermute | solution.py:41
  120.9 21.5 %copy-start.1 = (f32[2048,256]{1,0:T(8,128)S(1)}, f32[2048,256]{1,0:T(8,128)}, u32[]{:S(2)}) copy-start(f32[2048,256]{1,0:T(8,128)} %param.4) | copy-start | bytes 6291460
  120.9 21.5 %all-to-all-start.2 = ((f32[16,128,128]{2,1,0:T(8,128)}), f32[16,128,128]{2,1,0:T(8,128)}, u32[]{:S(2)}, u32[]{:S(2)}) async-start(f32[16,128,128]{2,1,0:T(8,128)} %broadcast_in_dim.13), calls=%async_computation.2 | async-start | bytes 2097152 | tf_op jit(solution)/shard_map/all_to_all | solution.py:19

commit v2 on v1

v2 whole, which is shorter than its diff:
```python
import jax
import jax.numpy as jnp
from jax import lax
from jax.experimental import pallas as pl
from jax.experimental.pallas import tpu as pltpu
from jax.sharding import Mesh, PartitionSpec as P

ROW = ("z", "core")
COL = ("y", "x")
ALL = ROW + COL
SLICE = 8
VMEM = 24 << 20
F32 = jnp.float32
NN = ((1,), (0,))
NT = ((1,), (1,))
TN = ((0,), (0,))


def exact(a, b, dims=NN):
    return lax.dot_general(
        a, b, (dims, ((), ())), precision=lax.Precision.HIGHEST, preferred_element_type=F32
    )


def split(a):
    high = a.astype(jnp.bfloat16)
    return high, (a - high.astype(F32)).astype(jnp.bfloat16)


def product(a, b, dims):
    def part(p, q):
        return lax.dot_general(p, q, (dims, ((), ())), preferred_element_type=F32)

    return part(a[0], b[0]) + (part(a[0], b[1]) + part(a[1], b[0]))


def copies(value, axis):
    return jnp.broadcast_to(value, (lax.axis_size(axis),) + value.shape)


def to_all(value, axis):
    return lax.all_to_all(copies(value, axis), axis, 0, 0)


def place(value, targets):
    nz, ncore, ncol = lax.axis_size("z"), lax.axis_size("core"), lax.axis_size(COL)

    def index(z, core, col):
        return (z * ncore + core) * ncol + col

    return [
        lax.ppermute(
            value,
            ALL,
            [
                (index(nz // 2, k, c), index(target, c % 2, (k * ncol + c) // 2))
                for k in range(ncore)
                for c in range(ncol)
            ],
        )
        for target in targets
    ]


def send_far(held):
    nz = lax.axis_size("z")
    return [lax.ppermute(held, "z", [(nz // 2, z)]) for z in (nz // 4, 3 * nz // 4, 0)]


def send_near(held):
    nz = lax.axis_size("z")
    step = nz // 8
    while step:
        held = held + lax.ppermute(held, "z", [(z, z + step) for z in range(0, nz, 2 * step)])
        step //= 2
    return held


def swapped(held):
    return lax.ppermute(held, "core", [(0, 1), (1, 0)])


def put_halves(core, mine, other, whole):
    half = mine.shape[0]
    whole[pl.ds(core * half, half), :] = mine[...]
    whole[pl.ds((1 - core) * half, half), :] = other[...]


def first_kernel(core_ref, slab, mine, other, out, whole):
    ncol, block = out.shape[:2]
    block -= SLICE
    put_halves(core_ref[0], mine, other, whole)
    right = split(whole[...])
    for i in range(ncol):
        out[i, :block, :] = product(split(slab[i * block : (i + 1) * block, :]), right, NN)


def cross_kernel(terms, rows, panel, other_av, out):
    ncol, block, nb = rows.shape
    cross = product(split(panel[...]), split(other_av[...]), TN)
    for i in range(ncol):
        cross = cross + product(split(rows[i]), split(terms[i, :block, :]), TN)
    out[:, block:, :] = cross.reshape(ncol, SLICE, nb)


def first(core, slab, rows, panel, other_av, mine, other):
    ncol, block, nb = rows.shape
    vmem = pl.BlockSpec(memory_space=pltpu.VMEM)
    shape = jax.ShapeDtypeStruct((ncol, block + SLICE, nb), F32)
    params = pltpu.CompilerParams(vmem_limit_bytes=VMEM)
    terms = pl.pallas_call(
        first_kernel,
        out_shape=shape,
        in_specs=[pl.BlockSpec(memory_space=pltpu.SMEM)] + [vmem] * 3,
        out_specs=vmem,
        scratch_shapes=[pltpu.VMEM((2 * block, nb), F32)],
        compiler_params=params,
        cost_estimate=pl.CostEstimate(
            flops=6*10**9, bytes_accessed=6 * slab.size, transcendentals=0
        ),
        name="first",
    )(core, slab, mine, other)
    return pl.pallas_call(
        cross_kernel,
        out_shape=shape,
        in_specs=[vmem] * 4,
        out_specs=vmem,
        input_output_aliases={0: 0},
        compiler_params=params,
        cost_estimate=pl.CostEstimate(
            flops=6 * rows.size * nb, bytes_accessed=8 * rows.size, transcendentals=0
        ),
        name="cross",
    )(terms, rows, panel, other_av)


def columns_kernel(core_ref, mine, other, wmine, wother, out):
    core, nb = core_ref[0], mine.shape[1]
    put_halves(core, wmine, wother, out.at[:, :nb])
    put_halves(core, mine, other, out.at[:, nb:])


def columns(core, *halves):
    half, nb = halves[0].shape
    vmem = pl.BlockSpec(memory_space=pltpu.VMEM)
    return pl.pallas_call(
        columns_kernel,
        out_shape=jax.ShapeDtypeStruct((2 * half, 2 * nb), F32),
        in_specs=[pl.BlockSpec(memory_space=pltpu.SMEM)] + [vmem] * 4,
        out_specs=vmem,
        cost_estimate=pl.CostEstimate(flops=6*10**9, bytes_accessed=32 * half * nb, transcendentals=0),
        name="columns",
    )(core, *halves)


def last_kernel(
    slab, rows, found, cross, panel, wmat, tfactor, pair,
    updated, correction, whole, right_high, right_low,
):
    nb = tfactor.shape[0]

    @pl.when(pl.program_id(0) == 0)
    def _():
        inner = exact(cross[...].reshape(nb, nb), tfactor[...])
        middle = exact(tfactor[...], inner, TN)
        correction[...] = wmat[...] - 0.5 * exact(panel[...], middle)
        both = 0.5 * (middle + middle.T)
        whole[...] = pair[...]
        whole[:, :nb] = whole[:, :nb] - exact(whole[:, nb:], both)
        right_high[...], right_low[...] = split(whole[...])

    step, block = found.shape[:2]
    left = jnp.concatenate(
        [rows[...].reshape(step * block, nb), found[...].reshape(step * block, nb)], axis=1
    )
    updated[...] = slab[...] - product(split(left), (right_high[...], right_low[...]), NT)


def last(slab, rows, found, panel, wmat, tfactor, pair):
    ncol, block, nb = rows.shape
    height, width = slab.shape
    step = 4

    def whole(*shape):
        return pl.BlockSpec(shape, lambda i: (0,) * len(shape))

    return pl.pallas_call(
        last_kernel,
        grid=(ncol // step,),
        out_shape=(
            jax.ShapeDtypeStruct(slab.shape, F32),
            jax.ShapeDtypeStruct((block, nb), F32),
        ),
        in_specs=[
            pl.BlockSpec((step * block, width), lambda i: (i, 0)),
            pl.BlockSpec((step, block, nb), lambda i: (i, 0, 0)),
            pl.BlockSpec((step, block, nb), lambda i: (i, 0, 0)),
            pl.BlockSpec((ncol, SLICE, nb), lambda i: (0, block // SLICE, 0)),
        ]
        + [whole(nb, nb)] * 3
        + [whole(width, 2 * nb)],
        out_specs=(pl.BlockSpec((step * block, width), lambda i: (i, 0)), whole(block, nb)),
        scratch_shapes=[
            pltpu.VMEM((width, 2 * nb), F32),
            pltpu.VMEM((width, 2 * nb), jnp.bfloat16),
            pltpu.VMEM((width, 2 * nb), jnp.bfloat16),
        ],
        compiler_params=pltpu.CompilerParams(vmem_limit_bytes=VMEM),
        cost_estimate=pl.CostEstimate(
            flops=12 * slab.size * nb, bytes_accessed=4 * (2 * slab.size + 2 * rows.size), transcendentals=0
        ),
        name="last",
    )(slab, rows, found, found, panel, wmat, tfactor, pair)


def on_device(slab, panel, tfactor, other_av):
    ncol = lax.axis_size(COL)
    block = panel.shape[0]
    core = lax.axis_index("core").astype(jnp.int32)[None]
    spread = copies(panel, COL)
    held = place(panel, (8,))[0]
    held, spread = lax.optimization_barrier((held, spread))
    rows = lax.all_to_all(spread, COL, 0, 0)
    held = held + sum(send_far(held))
    mine = send_near(held)
    other = swapped(mine)
    sent = first(core, slab, rows, panel, other_av, mine, other)
    summed = lax.all_to_all(sent, COL, 0, 0).sum(axis=0)
    wmat = exact(summed[:block] + other_av, tfactor)
    part = summed[block:]
    part = part + swapped(part)
    held = sum(place(wmat, (8, 12, 4, 0)))
    part = to_all(part, "z").sum(axis=0)
    found = to_all(jnp.concatenate([wmat, part], axis=0), COL)
    wmine = send_near(held)
    pair = columns(core, mine, other, wmine, swapped(wmine))
    return last(slab, rows, found, panel, wmat, tfactor, pair)


def solution(mesh):
    nrow, ncol = mesh.devices.shape
    grid = Mesh(mesh.devices.reshape(nrow // 2, 2, 4, ncol // 4), ALL)
    placed = (P(ROW, COL), P(ALL, None), P(), P(ALL, None))
    return jax.shard_map(
        on_device,
        mesh=grid,
        in_specs=placed,
        out_specs=(P(ROW, COL), P(ALL, None)),
        check_vma=False,
    )
```

time: 148 us -> 123 us (0.83)
  the two profiles are of different devices: /device:TPU:96 before, /device:TPU:1 now
where the time goes in v2:
time: 123 us; the launch traced here: 121 us
  starting transfers between devices  46.7 us (38%)
  waiting for transfers between devices  30.8 us (25%)
  blocking collectives  27 us (22%)
  local copies, waits for them, and re-layouts  8.42 us (7%)
  Pallas kernels  7.05 us (6%)
    all_to_all x1, blocking collectives, on_device(): summed = lax.all_to_all(sent, COL, 0, 0).sum(axis=0)  27 us
    all_to_all x2, starting transfers between devices, to_all(): return lax.all_to_all(copies(value, axis), axis, 0, 0)  14.8 us
    ppermute x3, waiting for transfers between devices, send_far(): lax.ppermute(held, 'z', [(nz // 2, z)])  14 us
    ppermute x3, starting transfers between devices, swapped(): return lax.ppermute(held, 'core', [(0, 1), (1, 0)])  11.2 us
    all_to_all x2, waiting for transfers between devices, to_all(): return lax.all_to_all(copies(value, axis), axis, 0, 0)  8.15 us
    all_to_all x1, starting transfers between devices, on_device(): rows = lax.all_to_all(spread, COL, 0, 0)  7.6 us
    ppermute x4, starting transfers between devices, send_near(): lax.ppermute(held, 'z', [(z, z + step) for z in range(0, nz, 2 * step)])  6.53 us
    ppermute x4, waiting for transfers between devices, send_near(): lax.ppermute(held, 'z', [(z, z + step) for z in range(0, nz, 2 * step)])  5.7 us
  transfers between devices with their start and end apart: 18, of which 9 were waited for; matrix products, arithmetic and copies ran while one was open for 1% of the time, Pallas kernels for 2%

profile of v2, /device:TPU:1, one launch (start us, length us, event | category | flops | bytes accessed | tf_op | source)
XLA Modules:
  0.0 121.2 jit_solution(3284787758209330370)
XLA Ops:
  0.6 0.7 collective-permute-start
  1.3 1.9 %broadcast_in_dim.12 = f32[16,128,128]{2,1,0:T(8,128)} broadcast(f32[128,128]{1,0:T(8,128)} %panel.3), dimensions={1,2} | broadcast | bytes 1114112 | tf_op jit(solution)/shard_map/broadcast_in_dim | solution.py:38
  3.2 1.3 %collective-permute-start.3 = (f32[128,128]{1,0:T(8,128)S(1)}, f32[128,128]{1,0:T(8,128)S(1)}, u32[]{:S(2)}, u32[]{:S(2)}) collective-permute-start(f32[128,128]{1,0:T(8,128)S(1)} %collective-permute-done), channel_id=1, source_target_pairs={{256,0},{257,1},{258,2},{259,3},{260,4},{261,5},{262,6},{263,7},{2... | collective-permute-start | bytes 196616 | tf_op jit(solution)/shard_map/ppermute | solution.py:67
  4.5 0.7 collective-permute-start.2
  5.9 7.6 %all-to-all-start = ((f32[16,128,128]{2,1,0:T(8,128)}), f32[16,128,128]{2,1,0:T(8,128)S(1)}, u32[]{:S(2)}, u32[]{:S(2)}) async-start(f32[16,128,128]{2,1,0:T(8,128)} %broadcast_in_dim.12), calls=%async_computation | async-start | bytes 2097152 | tf_op jit(solution)/shard_map/all_to_all | solution.py:223
  13.5 14.0 %collective-permute-done.3 = f32[128,128]{1,0:T(8,128)S(1)} collective-permute-done((f32[128,128]{1,0:T(8,128)S(1)}, f32[128,128]{1,0:T(8,128)S(1)}, u32[]{:S(2)}, u32[]{:S(2)}) %collective-permute-start.3) | collective-permute-done | bytes 65568 | tf_op jit(solution)/shard_map/ppermute | solution.py:67
  27.5 1.3 %collective-permute-start.4 = (f32[128,128]{1,0:T(8,128)S(1)}, f32[128,128]{1,0:T(8,128)S(1)}, u32[]{:S(2)}, u32[]{:S(2)}) collective-permute-start(f32[128,128]{1,0:T(8,128)S(1)} %add_add_fusion.1), channel_id=1, source_target_pairs={{0,64},{128,192},{256,320},{384,448},{1,65},{129,193},{257,321},{3... | collective-permute-start | bytes 196616 | tf_op jit(solution)/shard_map/ppermute | solution.py:74
  28.8 1.3 %collective-permute-done.4 = f32[128,128]{1,0:T(8,128)S(1)} collective-permute-done((f32[128,128]{1,0:T(8,128)S(1)}, f32[128,128]{1,0:T(8,128)S(1)}, u32[]{:S(2)}, u32[]{:S(2)}) %collective-permute-start.4) | collective-permute-done | bytes 65568 | tf_op jit(solution)/shard_map/ppermute | solution.py:74
  30.1 1.3 %collective-permute-start.5 = (f32[128,128]{1,0:T(8,128)S(1)}, f32[128,128]{1,0:T(8,128)S(1)}, u32[]{:S(2)}, u32[]{:S(2)}) collective-permute-start(f32[128,128]{1,0:T(8,128)S(1)} %add.39), channel_id=1, source_target_pairs={{0,32},{64,96},{128,160},{192,224},{256,288},{320,352},{384,416},{... | collective-permute-start | bytes 196616 | tf_op jit(solution)/shard_map/ppermute | solution.py:74
  31.4 1.3 %collective-permute-done.5 = f32[128,128]{1,0:T(8,128)S(1)} collective-permute-done((f32[128,128]{1,0:T(8,128)S(1)}, f32[128,128]{1,0:T(8,128)S(1)}, u32[]{:S(2)}, u32[]{:S(2)}) %collective-permute-start.5) | collective-permute-done | bytes 65568 | tf_op jit(solution)/shard_map/ppermute | solution.py:74
  32.7 1.9 %collective-permute-start.6 = (f32[128,128]{1,0:T(8,128)S(1)}, f32[128,128]{1,0:T(8,128)S(1)}, u32[]{:S(2)}, u32[]{:S(2)}) collective-permute-start(f32[128,128]{1,0:T(8,128)S(1)} %add.40.mine), channel_id=1, source_target_pairs={{0,16},{16,0},{1,17},{17,1},{2,18},{18,2},{3,19},{19,3},{4,20},{20... | collective-permute-start | bytes 196616 | tf_op jit(solution)/shard_map/ppermute | solution.py:80
  34.7 1.2 %collective-permute-done.6.other = f32[128,128]{1,0:T(8,128)S(1)} collective-permute-done((f32[128,128]{1,0:T(8,128)S(1)}, f32[128,128]{1,0:T(8,128)S(1)}, u32[]{:S(2)}, u32[]{:S(2)}) %collective-permute-start.6) | collective-permute-done | bytes 65568 | tf_op jit(solution)/shard_map/ppermute | solution.py:80
  35.9 1.6 %copy-done = f32[2048,256]{1,0:T(8,128)S(1)} copy-done((f32[2048,256]{1,0:T(8,128)S(1)}, f32[2048,256]{1,0:T(8,128)}, u32[]{:S(2)}) %copy-start) | copy-done | bytes 2097176
  37.5 1.0 first.1.terms
  39.2 27.0 %all_to_all.20 = f32[16,136,128]{2,1,0:T(8,128)S(1)} all-to-all(f32[16,136,128]{2,1,0:T(8,128)S(1)} %cross.1), channel_id=1, replica_groups=mesh['z'=16,'core'=2,'y'=4,'x'=4] {'y','x'}, dimensions={0} | all-to-all | bytes 2228224 | tf_op jit(solution)/shard_map/all_to_all | solution.py:228
  66.3 3.7 %collective-permute-start.7 = (f32[8,128]{1,0:T(8,128)S(1)}, f32[8,128]{1,0:T(8,128)S(1)}, u32[]{:S(2)}, u32[]{:S(2)}) collective-permute-start(f32[8,128]{1,0:T(8,128)S(1)} %slice.9), channel_id=1, source_target_pairs={{0,16},{16,0},{1,17},{17,1},{2,18},{18,2},{3,19},{19,3},{4,20},{20... | collective-permute-start | bytes 12296 | tf_op jit(solution)/shard_map/ppermute | solution.py:80
  70.0 0.8 collective-permute-done.7
  71.4 11.1 %all-to-all-start.2 = ((f32[16,8,128]{2,1,0:T(8,128)}), f32[16,8,128]{2,1,0:T(8,128)S(1)}, u32[]{:S(2)}, u32[]{:S(2)}) async-start(f32[16,8,128]{2,1,0:T(8,128)} %broadcast_in_dim.14), calls=%async_computation.2 | async-start | bytes 131072 | tf_op jit(solution)/shard_map/all_to_all | solution.py:42
  82.7 1.3 %collective-permute-start.11 = (f32[128,128]{1,0:T(8,128)S(1)}, f32[128,128]{1,0:T(8,128)S(1)}, u32[]{:S(2)}, u32[]{:S(2)}) collective-permute-start(f32[128,128]{1,0:T(8,128)S(1)} %fusion.wmat), channel_id=1, source_target_pairs={{256,0},{257,16},{258,1},{259,17},{260,2},{261,18},{262,3},{263,19... | collective-permute-start | bytes 196616 | tf_op jit(solution)/shard_map/ppermute | solution.py:52
  86.0 8.1 %all-to-all-done.2 = f32[16,8,128]{2,1,0:T(8,128)S(1)} async-done(((f32[16,8,128]{2,1,0:T(8,128)}), f32[16,8,128]{2,1,0:T(8,128)S(1)}, u32[]{:S(2)}, u32[]{:S(2)}) %all-to-all-start.2) | async-done | bytes 65568 | tf_op jit(solution)/shard_map/all_to_all | solution.py:42
  94.2 1.1 broadcast_in_dim.15
  95.3 3.7 %all-to-all-start.3 = ((f32[16,136,128]{2,1,0:T(8,128)}), f32[16,136,128]{2,1,0:T(8,128)S(1)}, u32[]{:S(2)}, u32[]{:S(2)}) async-start(f32[16,136,128]{2,1,0:T(8,128)} %broadcast_in_dim.15), calls=%async_computation.3 | async-start | bytes 2228224 | tf_op jit(solution)/shard_map/all_to_all | solution.py:42
  99.0 2.7 %collective-permute-start.12 = (f32[128,128]{1,0:T(8,128)S(1)}, f32[128,128]{1,0:T(8,128)S(1)}, u32[]{:S(2)}, u32[]{:S(2)}) collective-permute-start(f32[128,128]{1,0:T(8,128)S(1)} %add_add_fusion), channel_id=1, source_target_pairs={{0,64},{128,192},{256,320},{384,448},{1,65},{129,193},{257,321},{3... | collective-permute-start | bytes 196616 | tf_op jit(solution)/shard_map/ppermute | solution.py:74
  101.7 1.3 %collective-permute-done.12 = f32[128,128]{1,0:T(8,128)S(1)} collective-permute-done((f32[128,128]{1,0:T(8,128)S(1)}, f32[128,128]{1,0:T(8,128)S(1)}, u32[]{:S(2)}, u32[]{:S(2)}) %collective-permute-start.12) | collective-permute-done | bytes 65568 | tf_op jit(solution)/shard_map/ppermute | solution.py:74
  103.0 1.3 %collective-permute-start.13 = (f32[128,128]{1,0:T(8,128)S(1)}, f32[128,128]{1,0:T(8,128)S(1)}, u32[]{:S(2)}, u32[]{:S(2)}) collective-permute-start(f32[128,128]{1,0:T(8,128)S(1)} %add.46), channel_id=1, source_target_pairs={{0,32},{64,96},{128,160},{192,224},{256,288},{320,352},{384,416},{... | collective-permute-start | bytes 196616 | tf_op jit(solution)/shard_map/ppermute | solution.py:74
  104.3 1.8 %collective-permute-done.13 = f32[128,128]{1,0:T(8,128)S(1)} collective-permute-done((f32[128,128]{1,0:T(8,128)S(1)}, f32[128,128]{1,0:T(8,128)S(1)}, u32[]{:S(2)}, u32[]{:S(2)}) %collective-permute-start.13) | collective-permute-done | bytes 65568 | tf_op jit(solution)/shard_map/ppermute | solution.py:74
  106.1 5.6 %collective-permute-start.14 = (f32[128,128]{1,0:T(8,128)S(1)}, f32[128,128]{1,0:T(8,128)S(1)}, u32[]{:S(2)}, u32[]{:S(2)}) collective-permute-start(f32[128,128]{1,0:T(8,128)S(1)} %add.47.wmine), channel_id=1, source_target_pairs={{0,16},{16,0},{1,17},{17,1},{2,18},{18,2},{3,19},{19,3},{4,20},{20... | collective-permute-start | bytes 196616 | tf_op jit(solution)/shard_map/ppermute | solution.py:80
  111.8 0.9 collective-permute-done.14.wother
  113.3 1.7 %columns.1.pair = f32[256,256]{1,0:T(8,128)} custom-call(s32[1]{0:T(128)} %bitcast.core_ref, f32[128,128]{1,0:T(8,128)} %copy-done.6, f32[128,128]{1,0:T(8,128)} %copy-done.7, f32[128,128]{1,0:T(8,128)} %copy-done.8, f32[128,128]{1,0:T(8,128)} %copy-done.9), custom_call_target="tpu_custom_call" | custom-call | flops 6000000000 | bytes 524288 | tf_op jit(solution)/shard_map/columns/pallas_call | solution.py:146
  114.9 1.6 %copy-done.1 = f32[2048,256]{1,0:T(8,128)S(1)} copy-done((f32[2048,256]{1,0:T(8,128)S(1)}, f32[2048,256]{1,0:T(8,128)}, u32[]{:S(2)}) %copy-start.1) | copy-done | bytes 2097176
  116.5 0.9 copy-done.4
  117.5 3.8 %last.1 = (f32[2048,256]{1,0:T(8,128)}, f32[128,128]{1,0:T(8,128)}) custom-call(f32[2048,256]{1,0:T(8,128)S(1)} %copy-done.1, f32[16,128,128]{2,1,0:T(8,128)S(1)} %all-to-all-done.rows, f32[16,136,128]{2,1,0:T(8,128)S(1)} %all-to-all-done.3.found.cross, f32[16,136,128]{2,1,0:T(8,128)S(1)} %all-to-all-done.3.found.cross, f32[128,128]{1,0:T(8,128)S(1)} %copy-done.2, ...), custom_call_target="tpu_custom_call" | custom-call | flops 805306368 | bytes 6291456 | tf_op jit(solution)/shard_map/last/pallas_call | solution.py:187
  (44 shorter events, 5.0 us)
Async XLA Ops:
  0.6 0.7 collective-permute-start
  3.2 24.2 %collective-permute-start.3 = (f32[128,128]{1,0:T(8,128)S(1)}, f32[128,128]{1,0:T(8,128)S(1)}, u32[]{:S(2)}, u32[]{:S(2)}) collective-permute-start(f32[128,128]{1,0:T(8,128)S(1)} %collective-permute-done), channel_id=1, source_target_pairs={{256,0},{257,1},{258,2},{259,3},{260,4},{261,5},{262,6},{263,7},{2... | collective-permute-start | bytes 196616 | tf_op jit(solution)/shard_map/ppermute | solution.py:67
  4.5 22.9 %collective-permute-start.2 = (f32[128,128]{1,0:T(8,128)S(1)}, f32[128,128]{1,0:T(8,128)S(1)}, u32[]{:S(2)}, u32[]{:S(2)}) collective-permute-start(f32[128,128]{1,0:T(8,128)S(1)} %collective-permute-done), channel_id=1, source_target_pairs={{256,384},{257,385},{258,386},{259,387},{260,388},{261,389},{262,3... | collective-permute-start | bytes 196616 | tf_op jit(solution)/shard_map/ppermute | solution.py:67
  5.2 22.3 %collective-permute-start.1 = (f32[128,128]{1,0:T(8,128)S(1)}, f32[128,128]{1,0:T(8,128)S(1)}, u32[]{:S(2)}, u32[]{:S(2)}) collective-permute-start(f32[128,128]{1,0:T(8,128)S(1)} %collective-permute-done), channel_id=1, source_target_pairs={{256,128},{257,129},{258,130},{259,131},{260,132},{261,133},{262,1... | collective-permute-start | bytes 196616 | tf_op jit(solution)/shard_map/ppermute | solution.py:67
  5.9 32.7 %all-to-all-start = ((f32[16,128,128]{2,1,0:T(8,128)}), f32[16,128,128]{2,1,0:T(8,128)S(1)}, u32[]{:S(2)}, u32[]{:S(2)}) async-start(f32[16,128,128]{2,1,0:T(8,128)} %broadcast_in_dim.12), calls=%async_computation | async-start | bytes 2097152 | tf_op jit(solution)/shard_map/all_to_all | solution.py:223
  27.5 2.6 %collective-permute-start.4 = (f32[128,128]{1,0:T(8,128)S(1)}, f32[128,128]{1,0:T(8,128)S(1)}, u32[]{:S(2)}, u32[]{:S(2)}) collective-permute-start(f32[128,128]{1,0:T(8,128)S(1)} %add_add_fusion.1), channel_id=1, source_target_pairs={{0,64},{128,192},{256,320},{384,448},{1,65},{129,193},{257,321},{3... | collective-permute-start | bytes 196616 | tf_op jit(solution)/shard_map/ppermute | solution.py:74
  30.1 2.6 %collective-permute-start.5 = (f32[128,128]{1,0:T(8,128)S(1)}, f32[128,128]{1,0:T(8,128)S(1)}, u32[]{:S(2)}, u32[]{:S(2)}) collective-permute-start(f32[128,128]{1,0:T(8,128)S(1)} %add.39), channel_id=1, source_target_pairs={{0,32},{64,96},{128,160},{192,224},{256,288},{320,352},{384,416},{... | collective-permute-start | bytes 196616 | tf_op jit(solution)/shard_map/ppermute | solution.py:74
  32.7 5.8 %copy-start.6 = (f32[128,128]{1,0:T(8,128)}, f32[128,128]{1,0:T(8,128)S(1)}, u32[]{:S(2)}) copy-start(f32[128,128]{1,0:T(8,128)S(1)} %add.40.mine) | copy-start | bytes 196612
  32.7 3.1 %collective-permute-start.6 = (f32[128,128]{1,0:T(8,128)S(1)}, f32[128,128]{1,0:T(8,128)S(1)}, u32[]{:S(2)}, u32[]{:S(2)}) collective-permute-start(f32[128,128]{1,0:T(8,128)S(1)} %add.40.mine), channel_id=1, source_target_pairs={{0,16},{16,0},{1,17},{17,1},{2,18},{18,2},{3,19},{19,3},{4,20},{20... | collective-permute-start | bytes 196616 | tf_op jit(solution)/shard_map/ppermute | solution.py:80
  35.9 2.6 %copy-start.7 = (f32[128,128]{1,0:T(8,128)}, f32[128,128]{1,0:T(8,128)S(1)}, u32[]{:S(2)}) copy-start(f32[128,128]{1,0:T(8,128)S(1)} %collective-permute-done.6.other) | copy-start | bytes 196612
  35.9 1.6 %copy-start = (f32[2048,256]{1,0:T(8,128)S(1)}, f32[2048,256]{1,0:T(8,128)}, u32[]{:S(2)}) copy-start(f32[2048,256]{1,0:T(8,128)} %slab.3) | copy-start | bytes 6291460
  37.5 1.0 copy-start.2
  37.5 1.0 copy-start.5
  66.2 16.3 %copy-start.3 = (f32[128,128]{1,0:T(8,128)S(1)}, f32[128,128]{1,0:T(8,128)}, u32[]{:S(2)}) copy-start(f32[128,128]{1,0:T(8,128)} %tfactor.1) | copy-start | bytes 196612
  66.3 4.5 %collective-permute-start.7 = (f32[8,128]{1,0:T(8,128)S(1)}, f32[8,128]{1,0:T(8,128)S(1)}, u32[]{:S(2)}, u32[]{:S(2)}) collective-permute-start(f32[8,128]{1,0:T(8,128)S(1)} %slice.9), channel_id=1, source_target_pairs={{0,16},{16,0},{1,17},{17,1},{2,18},{18,2},{3,19},{19,3},{4,20},{20... | collective-permute-start | bytes 12296 | tf_op jit(solution)/shard_map/ppermute | solution.py:80
  71.4 22.8 %all-to-all-start.2 = ((f32[16,8,128]{2,1,0:T(8,128)}), f32[16,8,128]{2,1,0:T(8,128)S(1)}, u32[]{:S(2)}, u32[]{:S(2)}) async-start(f32[16,8,128]{2,1,0:T(8,128)} %broadcast_in_dim.14), calls=%async_computation.2 | async-start | bytes 131072 | tf_op jit(solution)/shard_map/all_to_all | solution.py:42
  82.7 16.3 %collective-permute-start.11 = (f32[128,128]{1,0:T(8,128)S(1)}, f32[128,128]{1,0:T(8,128)S(1)}, u32[]{:S(2)}, u32[]{:S(2)}) collective-permute-start(f32[128,128]{1,0:T(8,128)S(1)} %fusion.wmat), channel_id=1, source_target_pairs={{256,0},{257,16},{258,1},{259,17},{260,2},{261,18},{262,3},{263,19... | collective-permute-start | bytes 196616 | tf_op jit(solution)/shard_map/ppermute | solution.py:52
  84.0 15.0 %collective-permute-start.10 = (f32[128,128]{1,0:T(8,128)S(1)}, f32[128,128]{1,0:T(8,128)S(1)}, u32[]{:S(2)}, u32[]{:S(2)}) collective-permute-start(f32[128,128]{1,0:T(8,128)S(1)} %fusion.wmat), channel_id=1, source_target_pairs={{256,128},{257,144},{258,129},{259,145},{260,130},{261,146},{262,1... | collective-permute-start | bytes 196616 | tf_op jit(solution)/shard_map/ppermute | solution.py:52
  84.7 14.3 %collective-permute-start.9 = (f32[128,128]{1,0:T(8,128)S(1)}, f32[128,128]{1,0:T(8,128)S(1)}, u32[]{:S(2)}, u32[]{:S(2)}) collective-permute-start(f32[128,128]{1,0:T(8,128)S(1)} %fusion.wmat), channel_id=1, source_target_pairs={{256,384},{257,400},{258,385},{259,401},{260,386},{261,402},{262,3... | collective-permute-start | bytes 196616 | tf_op jit(solution)/shard_map/ppermute | solution.py:52
  85.4 13.7 %collective-permute-start.8 = (f32[128,128]{1,0:T(8,128)S(1)}, f32[128,128]{1,0:T(8,128)S(1)}, u32[]{:S(2)}, u32[]{:S(2)}) collective-permute-start(f32[128,128]{1,0:T(8,128)S(1)} %fusion.wmat), channel_id=1, source_target_pairs={{256,256},{257,272},{258,257},{259,273},{260,258},{261,274},{262,2... | collective-permute-start | bytes 196616 | tf_op jit(solution)/shard_map/ppermute | solution.py:52
  95.3 19.6 %all-to-all-start.3 = ((f32[16,136,128]{2,1,0:T(8,128)}), f32[16,136,128]{2,1,0:T(8,128)S(1)}, u32[]{:S(2)}, u32[]{:S(2)}) async-start(f32[16,136,128]{2,1,0:T(8,128)} %broadcast_in_dim.15), calls=%async_computation.3 | async-start | bytes 2228224 | tf_op jit(solution)/shard_map/all_to_all | solution.py:42
  99.0 4.0 %collective-permute-start.12 = (f32[128,128]{1,0:T(8,128)S(1)}, f32[128,128]{1,0:T(8,128)S(1)}, u32[]{:S(2)}, u32[]{:S(2)}) collective-permute-start(f32[128,128]{1,0:T(8,128)S(1)} %add_add_fusion), channel_id=1, source_target_pairs={{0,64},{128,192},{256,320},{384,448},{1,65},{129,193},{257,321},{3... | collective-permute-start | bytes 196616 | tf_op jit(solution)/shard_map/ppermute | solution.py:74
  103.0 3.1 %collective-permute-start.13 = (f32[128,128]{1,0:T(8,128)S(1)}, f32[128,128]{1,0:T(8,128)S(1)}, u32[]{:S(2)}, u32[]{:S(2)}) collective-permute-start(f32[128,128]{1,0:T(8,128)S(1)} %add.46), channel_id=1, source_target_pairs={{0,32},{64,96},{128,160},{192,224},{256,288},{320,352},{384,416},{... | collective-permute-start | bytes 196616 | tf_op jit(solution)/shard_map/ppermute | solution.py:74
  106.1 6.5 %copy-start.8 = (f32[128,128]{1,0:T(8,128)}, f32[128,128]{1,0:T(8,128)S(1)}, u32[]{:S(2)}) copy-start(f32[128,128]{1,0:T(8,128)S(1)} %add.47.wmine) | copy-start | bytes 196612
  106.1 6.5 %collective-permute-start.14 = (f32[128,128]{1,0:T(8,128)S(1)}, f32[128,128]{1,0:T(8,128)S(1)}, u32[]{:S(2)}, u32[]{:S(2)}) collective-permute-start(f32[128,128]{1,0:T(8,128)S(1)} %add.47.wmine), channel_id=1, source_target_pairs={{0,16},{16,0},{1,17},{17,1},{2,18},{18,2},{3,19},{19,3},{4,20},{20... | collective-permute-start | bytes 196616 | tf_op jit(solution)/shard_map/ppermute | solution.py:80
  112.6 0.6 copy-start.9
  114.9 1.6 %copy-start.1 = (f32[2048,256]{1,0:T(8,128)S(1)}, f32[2048,256]{1,0:T(8,128)}, u32[]{:S(2)}) copy-start(f32[2048,256]{1,0:T(8,128)} %slab.3) | copy-start | bytes 6291460
  116.5 0.9 copy-start.4

commit v3 on v2

--- a/solution.py
+++ b/solution.py
@@ -9,7 +9,8 @@
 COL = ("y", "x")
 ALL = ROW + COL
 SLICE = 8
-VMEM = 24 << 20
+VMEM = 16 << 20
+PARTS = 4
 F32 = jnp.float32
 NN = ((1,), (0,))
 NT = ((1,), (1,))
@@ -134,6 +135,50 @@
     )(terms, rows, panel, other_av)
 
 
+def summed_kernel(terms, other_av, tfactor, wmat, part):
+    block = wmat.shape[0]
+    total = terms[0]
+    for i in range(1, terms.shape[0]):
+        total = total + terms[i]
+    wmat[...] = exact(total[:block] + other_av[...], tfactor[...])
+    part[...] = total[block:]
+
+
+def summed(terms, other_av, tfactor):
+    vmem = pl.BlockSpec(memory_space=pltpu.VMEM)
+    return pl.pallas_call(
+        summed_kernel,
+        out_shape=(
+            jax.ShapeDtypeStruct(other_av.shape, F32),
+            jax.ShapeDtypeStruct((SLICE, other_av.shape[1]), F32),
+        ),
+        in_specs=[vmem] * 3,
+        out_specs=(vmem, vmem),
+        compiler_params=pltpu.CompilerParams(vmem_limit_bytes=VMEM),
+        cost_estimate=pl.CostEstimate(
+            flops=12 * other_av.size * tfactor.shape[0], bytes_accessed=4 * terms.size, transcendentals=0
+        ),
+        name="summed",
+    )(terms, other_av, tfactor)
+
+
+def relayed_kernel(got, out):
+    out[...] = got[...]
+
+
+def relayed(got):
+    vmem = pl.BlockSpec(memory_space=pltpu.VMEM)
+    return pl.pallas_call(
+        relayed_kernel,
+        out_shape=jax.ShapeDtypeStruct(got.shape, F32),
+        in_specs=[vmem],
+        out_specs=vmem,
+        compiler_params=pltpu.CompilerParams(vmem_limit_bytes=VMEM),
+        cost_estimate=pl.CostEstimate(flops=60*10**9, bytes_accessed=8 * got.size, transcendentals=0),
+        name="relayed",
+    )(got)
+
+
 def columns_kernel(core_ref, mine, other, wmine, wother, out):
     core, nb = core_ref[0], mine.shape[1]
     put_halves(core, wmine, wother, out.at[:, :nb])
@@ -148,89 +193,78 @@
         out_shape=jax.ShapeDtypeStruct((2 * half, 2 * nb), F32),
         in_specs=[pl.BlockSpec(memory_space=pltpu.SMEM)] + [vmem] * 4,
         out_specs=vmem,
+        compiler_params=pltpu.CompilerParams(vmem_limit_bytes=VMEM),
         cost_estimate=pl.CostEstimate(flops=6*10**9, bytes_accessed=32 * half * nb, transcendentals=0),
         name="columns",
     )(core, *halves)
 
 
 def last_kernel(
-    slab, rows, found, cross, panel, wmat, tfactor, pair,
-    updated, correction, whole, right_high, right_low,
+    slab, rows, found, panel, wmat, tfactor, pair, updated, correction, result, sems
 ):
-    nb = tfactor.shape[0]
-
-    @pl.when(pl.program_id(0) == 0)
-    def _():
-        inner = exact(cross[...].reshape(nb, nb), tfactor[...])
-        middle = exact(tfactor[...], inner, TN)
-        correction[...] = wmat[...] - 0.5 * exact(panel[...], middle)
-        both = 0.5 * (middle + middle.T)
-        whole[...] = pair[...]
-        whole[:, :nb] = whole[:, :nb] - exact(whole[:, nb:], both)
-        right_high[...], right_low[...] = split(whole[...])
-
-    step, block = found.shape[:2]
-    left = jnp.concatenate(
-        [rows[...].reshape(step * block, nb), found[...].reshape(step * block, nb)], axis=1
-    )
-    updated[...] = slab[...] - product(split(left), (right_high[...], right_low[...]), NT)
+    ncol, block, nb = rows.shape
+    factor = split(tfactor[...])
+    inner = product(split(found[:, block:, :].reshape(nb, nb)), factor, NN)
+    middle = product(factor, split(inner), TN)
+    both = 0.5 * (middle + middle.T)
+    right = pair[...]
+    columns_v = right[:, nb:]
+    turned = right[:, :nb] - product(split(columns_v), split(both), NN)
+    right = split(jnp.concatenate([turned, columns_v], axis=1))
+    size = slab.shape[0] // PARTS
+    step = ncol // PARTS
+    stores = []
+    for i in range(PARTS):
+        here, part = pl.ds(i * size, size), slice(i * step, (i + 1) * step)
+        left = jnp.concatenate(
+            [rows[part].reshape(size, nb), found[part, :block, :].reshape(size, nb)], axis=1
+        )
+        result[here, :] = slab[here, :] - product(split(left), right, NT)
+        stores.append(pltpu.make_async_copy(result.at[here, :], updated.at[here, :], sems.at[i]))
+        stores[-1].start()
+    correction[...] = wmat[...] - 0.5 * product(split(panel[...]), split(middle), NN)
+    for store in stores:
+        store.wait()
 
 
 def last(slab, rows, found, panel, wmat, tfactor, pair):
-    ncol, block, nb = rows.shape
-    height, width = slab.shape
-    step = 4
-
-    def whole(*shape):
-        return pl.BlockSpec(shape, lambda i: (0,) * len(shape))
-
+    vmem = pl.BlockSpec(memory_space=pltpu.VMEM)
     return pl.pallas_call(
         last_kernel,
-        grid=(ncol // step,),
         out_shape=(
             jax.ShapeDtypeStruct(slab.shape, F32),
-            jax.ShapeDtypeStruct((block, nb), F32),
-        ),
-        in_specs=[
-            pl.BlockSpec((step * block, width), lambda i: (i, 0)),
-            pl.BlockSpec((step, block, nb), lambda i: (i, 0, 0)),
-            pl.BlockSpec((step, block, nb), lambda i: (i, 0, 0)),
-            pl.BlockSpec((ncol, SLICE, nb), lambda i: (0, block // SLICE, 0)),
-        ]
-        + [whole(nb, nb)] * 3
-        + [whole(width, 2 * nb)],
-        out_specs=(pl.BlockSpec((step * block, width), lambda i: (i, 0)), whole(block, nb)),
-        scratch_shapes=[
-            pltpu.VMEM((width, 2 * nb), F32),
-            pltpu.VMEM((width, 2 * nb), jnp.bfloat16),
-            pltpu.VMEM((width, 2 * nb), jnp.bfloat16),
-        ],
-        compiler_params=pltpu.CompilerParams(vmem_limit_bytes=VMEM),
-        cost_estimate=pl.CostEstimate(
-            flops=12 * slab.size * nb, bytes_accessed=4 * (2 * slab.size + 2 * rows.size), transcendentals=0
+            jax.ShapeDtypeStruct(wmat.shape, F32),
+        ),
+        in_specs=[vmem] * 7,
+        out_specs=(pl.BlockSpec(memory_space=pl.ANY), vmem),
+        scratch_shapes=[pltpu.VMEM(slab.shape, F32), pltpu.SemaphoreType.DMA((PARTS,))],
+        compiler_params=pltpu.CompilerParams(vmem_limit_bytes=VMEM),
+        cost_estimate=pl.CostEstimate(
+            flops=12 * slab.size * wmat.shape[1],
+            bytes_accessed=4 * (2 * slab.size + 2 * rows.size),
+            transcendentals=0,
         ),
         name="last",
-    )(slab, rows, found, found, panel, wmat, tfactor, pair)
+    )(slab, rows, found, panel, wmat, tfactor, pair)
 
 
 def on_device(slab, panel, tfactor, other_av):
     ncol = lax.axis_size(COL)
     block = panel.shape[0]
     core = lax.axis_index("core").astype(jnp.int32)[None]
-    spread = copies(panel, COL)
-    held = place(panel, (8,))[0]
-    held, spread = lax.optimization_barrier((held, spread))
+    tied, spread = lax.optimization_barrier((panel, copies(panel, COL)))
     rows = lax.all_to_all(spread, COL, 0, 0)
-    held = held + sum(send_far(held))
+    held = sum(place(tied, (8, 12, 4, 0)))
     mine = send_near(held)
     other = swapped(mine)
     sent = first(core, slab, rows, panel, other_av, mine, other)
-    summed = lax.all_to_all(sent, COL, 0, 0).sum(axis=0)
-    wmat = exact(summed[:block] + other_av, tfactor)
-    part = summed[block:]
+    wmat, part = summed(lax.all_to_all(sent, COL, 0, 0), other_av, tfactor)
     part = part + swapped(part)
-    held = sum(place(wmat, (8, 12, 4, 0)))
-    part = to_all(part, "z").sum(axis=0)
+    early = relayed(sum(place(wmat, (12, 4, 0))))
+    held = early + place(wmat, (8,))[0]
+    part = lax.all_to_all(
+        copies(part, "z"), "z", 0, 0, axis_index_groups=[[(i + 8) % 16 for i in range(16)]]
+    ).sum(axis=0)
     found = to_all(jnp.concatenate([wmat, part], axis=0), COL)
     wmine = send_near(held)
     pair = columns(core, mine, other, wmine, swapped(wmine))

time: 123 us -> 117 us (0.951)
  starting transfers between devices: 46.7 us -> 56.9 us
  waiting for transfers between devices: 30.8 us -> 22.9 us
  blocking collectives: 27 us -> 23.5 us
  Pallas kernels: 7.05 us -> 5.23 us
  local copies, waits for them, and re-layouts: 8.42 us -> 6.87 us
    all_to_all x0 -> x1, starting transfers between devices: none -> 16.4 us  [on_device(): lax.all_to_all(copies(part, 'z'), 'z', 0, 0, axis_index_groups=[[(i + 8)...]
    ppermute x3 -> x0, waiting for transfers between devices: 14 us -> none  [send_far(): lax.ppermute(held, 'z', [(nz // 2, z)])]
    all_to_all x2 -> x1, starting transfers between devices: 14.8 us -> 4.59 us  [to_all(): return lax.all_to_all(copies(value, axis), axis, 0, 0)]
    ppermute x5 -> x8, waiting for transfers between devices: 0.01 us -> 8.18 us  [place(): lax.ppermute(value, ALL, [(index(nz // 2, k, c), index(target, c % 2, (k...]
    all_to_all x2 -> x1, waiting for transfers between devices: 8.15 us -> 3.03 us  [to_all(): return lax.all_to_all(copies(value, axis), axis, 0, 0)]
    all_to_all x1, blocking collectives: 27 us -> 23.5 us  [on_device(): wmat, part = summed(lax.all_to_all(sent, COL, 0, 0), other_av, tfactor)]
    all_to_all x0 -> x1, waiting for transfers between devices: none -> 3.41 us  [on_device(): lax.all_to_all(copies(part, 'z'), 'z', 0, 0, axis_index_groups=[[(i + 8)...]
    ppermute x3, starting transfers between devices: 11.2 us -> 14.6 us  [swapped(): return lax.ppermute(held, 'core', [(0, 1), (1, 0)])]
  transfers between devices with their start and end apart: 18 -> 18, of which waited for: 9 -> 10; matrix products, arithmetic and copies ran while one was open for 1% -> 2% of each run, Pallas kernels for 2% -> 1%
where the time goes in v3:
time: 117 us; the launch traced here: 116 us
  starting transfers between devices  56.9 us (49%)
  blocking collectives  23.5 us (20%)
  waiting for transfers between devices  22.9 us (20%)
  local copies, waits for them, and re-layouts  6.87 us (6%)
  Pallas kernels  5.23 us (4%)
    all_to_all x1, blocking collectives, on_device(): wmat, part = summed(lax.all_to_all(sent, COL, 0, 0), other_av, tfactor)  23.5 us
    all_to_all x1, starting transfers between devices, on_device(): lax.all_to_all(copies(part, 'z'), 'z', 0, 0, axis_index_groups=[[(i + 8)...  16.4 us
    ppermute x3, starting transfers between devices, swapped(): return lax.ppermute(held, 'core', [(0, 1), (1, 0)])  14.6 us
    ppermute x8, waiting for transfers between devices, place(): lax.ppermute(value, ALL, [(index(nz // 2, k, c), index(target, c % 2, (k...  8.18 us
    all_to_all x1, starting transfers between devices, on_device(): rows = lax.all_to_all(spread, COL, 0, 0)  7.6 us
    ppermute x4, starting transfers between devices, send_near(): lax.ppermute(held, 'z', [(z, z + step) for z in range(0, nz, 2 * step)])  7.14 us
    ppermute x8, starting transfers between devices, place(): lax.ppermute(value, ALL, [(index(nz // 2, k, c), index(target, c % 2, (k...  6.55 us
    ppermute x4, waiting for transfers between devices, send_near(): lax.ppermute(held, 'z', [(z, z + step) for z in range(0, nz, 2 * step)])  5.78 us
  transfers between devices with their start and end apart: 18, of which 10 were waited for; matrix products, arithmetic and copies ran while one was open for 2% of the time, Pallas kernels for 1%

profile of v3, /device:TPU:1, one launch (start us, length us, event | category | flops | bytes accessed | tf_op | source)
XLA Modules:
  0.0 116.5 jit_solution(7158499214729931755)
XLA Ops:
  0.6 2.0 %broadcast_in_dim.12 = f32[16,128,128]{2,1,0:T(8,128)} broadcast(f32[128,128]{1,0:T(8,128)} %panel.3), dimensions={1,2} | broadcast | bytes 1114112 | tf_op jit(solution)/shard_map/broadcast_in_dim | solution.py:39
  2.6 1.3 %collective-permute-start.3 = (f32[128,128]{1,0:T(8,128)S(1)}, f32[128,128]{1,0:T(8,128)S(1)}, u32[]{:S(2)}, u32[]{:S(2)}) collective-permute-start(f32[128,128]{1,0:T(8,128)S(1)} %copy-done.2), channel_id=1, source_target_pairs={{256,0},{257,16},{258,1},{259,17},{260,2},{261,18},{262,3},{263,19... | collective-permute-start | bytes 196616 | tf_op jit(solution)/shard_map/ppermute | solution.py:53
  4.6 0.7 collective-permute-start.1
  5.2 0.7 collective-permute-start
  5.9 7.6 %all-to-all-start = ((f32[16,128,128]{2,1,0:T(8,128)}), f32[16,128,128]{2,1,0:T(8,128)S(1)}, u32[]{:S(2)}, u32[]{:S(2)}) async-start(f32[16,128,128]{2,1,0:T(8,128)} %broadcast_in_dim.12), calls=%async_computation | async-start | bytes 2097152 | tf_op jit(solution)/shard_map/all_to_all | solution.py:256
  13.5 8.2 %collective-permute-done.3 = f32[128,128]{1,0:T(8,128)S(1)} collective-permute-done((f32[128,128]{1,0:T(8,128)S(1)}, f32[128,128]{1,0:T(8,128)S(1)}, u32[]{:S(2)}, u32[]{:S(2)}) %collective-permute-start.3) | collective-permute-done | bytes 65568 | tf_op jit(solution)/shard_map/ppermute | solution.py:53
  21.7 1.3 %collective-permute-start.4 = (f32[128,128]{1,0:T(8,128)S(1)}, f32[128,128]{1,0:T(8,128)S(1)}, u32[]{:S(2)}, u32[]{:S(2)}) collective-permute-start(f32[128,128]{1,0:T(8,128)S(1)} %add_add_fusion.1), channel_id=1, source_target_pairs={{0,64},{128,192},{256,320},{384,448},{1,65},{129,193},{257,321},{3... | collective-permute-start | bytes 196616 | tf_op jit(solution)/shard_map/ppermute | solution.py:75
  23.0 1.3 %collective-permute-done.4 = f32[128,128]{1,0:T(8,128)S(1)} collective-permute-done((f32[128,128]{1,0:T(8,128)S(1)}, f32[128,128]{1,0:T(8,128)S(1)}, u32[]{:S(2)}, u32[]{:S(2)}) %collective-permute-start.4) | collective-permute-done | bytes 65568 | tf_op jit(solution)/shard_map/ppermute | solution.py:75
  24.3 1.3 %collective-permute-start.5 = (f32[128,128]{1,0:T(8,128)S(1)}, f32[128,128]{1,0:T(8,128)S(1)}, u32[]{:S(2)}, u32[]{:S(2)}) collective-permute-start(f32[128,128]{1,0:T(8,128)S(1)} %add.36), channel_id=1, source_target_pairs={{0,32},{64,96},{128,160},{192,224},{256,288},{320,352},{384,416},{... | collective-permute-start | bytes 196616 | tf_op jit(solution)/shard_map/ppermute | solution.py:75
  25.6 1.7 %collective-permute-done.5 = f32[128,128]{1,0:T(8,128)S(1)} collective-permute-done((f32[128,128]{1,0:T(8,128)S(1)}, f32[128,128]{1,0:T(8,128)S(1)}, u32[]{:S(2)}, u32[]{:S(2)}) %collective-permute-start.5) | collective-permute-done | bytes 65568 | tf_op jit(solution)/shard_map/ppermute | solution.py:75
  27.3 5.7 %collective-permute-start.6 = (f32[128,128]{1,0:T(8,128)S(1)}, f32[128,128]{1,0:T(8,128)S(1)}, u32[]{:S(2)}, u32[]{:S(2)}) collective-permute-start(f32[128,128]{1,0:T(8,128)S(1)} %add.37.mine), channel_id=1, source_target_pairs={{0,16},{16,0},{1,17},{17,1},{2,18},{18,2},{3,19},{19,3},{4,20},{20... | collective-permute-start | bytes 196616 | tf_op jit(solution)/shard_map/ppermute | solution.py:81
  33.1 0.9 collective-permute-done.6.other
  33.9 1.6 %copy-done = f32[2048,256]{1,0:T(8,128)S(1)} copy-done((f32[2048,256]{1,0:T(8,128)S(1)}, f32[2048,256]{1,0:T(8,128)}, u32[]{:S(2)}) %copy-start) | copy-done | bytes 2097176
  35.5 1.0 first.1.terms
  37.2 23.5 %all_to_all.20.terms = f32[16,136,128]{2,1,0:T(8,128)S(1)} all-to-all(f32[16,136,128]{2,1,0:T(8,128)S(1)} %cross.1), channel_id=1, replica_groups=mesh['z'=16,'core'=2,'y'=4,'x'=4] {'y','x'}, dimensions={0} | all-to-all | bytes 2228224 | tf_op jit(solution)/shard_map/all_to_all | solution.py:261
  60.9 1.3 %collective-permute-start.10 = (f32[128,128]{1,0:T(8,128)S(1)}, f32[128,128]{1,0:T(8,128)S(1)}, u32[]{:S(2)}, u32[]{:S(2)}) collective-permute-start(f32[128,128]{1,0:T(8,128)S(1)} %get-tuple-element.8.wmat), channel_id=1, source_target_pairs={{256,0},{257,16},{258,1},{259,17},{260,2},{261,18},{262,3},{263,19... | collective-permute-start | bytes 196616 | tf_op jit(solution)/shard_map/ppermute | solution.py:53
  62.2 0.7 collective-permute-start.9
  63.6 3.7 %collective-permute-start.7 = (f32[8,128]{1,0:T(8,128)S(1)}, f32[8,128]{1,0:T(8,128)S(1)}, u32[]{:S(2)}, u32[]{:S(2)}) collective-permute-start(f32[8,128]{1,0:T(8,128)S(1)} %get-tuple-element.9), channel_id=1, source_target_pairs={{0,16},{16,0},{1,17},{17,1},{2,18},{18,2},{3,19},{19,3},{4,20},{20... | collective-permute-start | bytes 12296 | tf_op jit(solution)/shard_map/ppermute | solution.py:81
  67.3 0.8 collective-permute-done.7
  68.7 16.4 %all-to-all-start.2 = ((f32[16,8,128]{2,1,0:T(8,128)}), f32[16,8,128]{2,1,0:T(8,128)S(1)}, u32[]{:S(2)}, u32[]{:S(2)}) async-start(f32[16,8,128]{2,1,0:T(8,128)} %broadcast_in_dim.14), calls=%async_computation.2 | async-start | bytes 131072 | tf_op jit(solution)/shard_map/all_to_all | solution.py:265
  85.8 3.4 %all-to-all-done.2 = f32[16,8,128]{2,1,0:T(8,128)S(1)} async-done(((f32[16,8,128]{2,1,0:T(8,128)}), f32[16,8,128]{2,1,0:T(8,128)S(1)}, u32[]{:S(2)}, u32[]{:S(2)}) %all-to-all-start.2) | async-done | bytes 65568 | tf_op jit(solution)/shard_map/all_to_all | solution.py:265
  89.3 1.1 broadcast_in_dim.15
  90.3 4.6 %all-to-all-start.3 = ((f32[16,136,128]{2,1,0:T(8,128)}), f32[16,136,128]{2,1,0:T(8,128)S(1)}, u32[]{:S(2)}, u32[]{:S(2)}) async-start(f32[16,136,128]{2,1,0:T(8,128)} %broadcast_in_dim.15), calls=%async_computation.3 | async-start | bytes 2228224 | tf_op jit(solution)/shard_map/all_to_all | solution.py:43
  95.0 3.3 %collective-permute-start.12 = (f32[128,128]{1,0:T(8,128)S(1)}, f32[128,128]{1,0:T(8,128)S(1)}, u32[]{:S(2)}, u32[]{:S(2)}) collective-permute-start(f32[128,128]{1,0:T(8,128)S(1)} %add.41), channel_id=1, source_target_pairs={{0,64},{128,192},{256,320},{384,448},{1,65},{129,193},{257,321},{3... | collective-permute-start | bytes 196616 | tf_op jit(solution)/shard_map/ppermute | solution.py:75
  98.3 1.3 %collective-permute-done.12 = f32[128,128]{1,0:T(8,128)S(1)} collective-permute-done((f32[128,128]{1,0:T(8,128)S(1)}, f32[128,128]{1,0:T(8,128)S(1)}, u32[]{:S(2)}, u32[]{:S(2)}) %collective-permute-start.12) | collective-permute-done | bytes 65568 | tf_op jit(solution)/shard_map/ppermute | solution.py:75
  99.6 1.3 %collective-permute-start.13 = (f32[128,128]{1,0:T(8,128)S(1)}, f32[128,128]{1,0:T(8,128)S(1)}, u32[]{:S(2)}, u32[]{:S(2)}) collective-permute-start(f32[128,128]{1,0:T(8,128)S(1)} %add.42), channel_id=1, source_target_pairs={{0,32},{64,96},{128,160},{192,224},{256,288},{320,352},{384,416},{... | collective-permute-start | bytes 196616 | tf_op jit(solution)/shard_map/ppermute | solution.py:75
  100.9 1.5 %collective-permute-done.13 = f32[128,128]{1,0:T(8,128)S(1)} collective-permute-done((f32[128,128]{1,0:T(8,128)S(1)}, f32[128,128]{1,0:T(8,128)S(1)}, u32[]{:S(2)}, u32[]{:S(2)}) %collective-permute-start.13) | collective-permute-done | bytes 65568 | tf_op jit(solution)/shard_map/ppermute | solution.py:75
  102.4 5.2 %collective-permute-start.14 = (f32[128,128]{1,0:T(8,128)S(1)}, f32[128,128]{1,0:T(8,128)S(1)}, u32[]{:S(2)}, u32[]{:S(2)}) collective-permute-start(f32[128,128]{1,0:T(8,128)S(1)} %add.43.wmine), channel_id=1, source_target_pairs={{0,16},{16,0},{1,17},{17,1},{2,18},{18,2},{3,19},{19,3},{4,20},{20... | collective-permute-start | bytes 196616 | tf_op jit(solution)/shard_map/ppermute | solution.py:81
  107.6 0.9 collective-permute-done.14.wother
  108.5 3.0 %all-to-all-done.3.found = f32[16,136,128]{2,1,0:T(8,128)S(1)} async-done(((f32[16,136,128]{2,1,0:T(8,128)}), f32[16,136,128]{2,1,0:T(8,128)S(1)}, u32[]{:S(2)}, u32[]{:S(2)}) %all-to-all-start.3) | async-done | bytes 1114144 | tf_op jit(solution)/shard_map/all_to_all | solution.py:43
  111.5 1.6 %copy-done.1 = f32[2048,256]{1,0:T(8,128)S(1)} copy-done((f32[2048,256]{1,0:T(8,128)S(1)}, f32[2048,256]{1,0:T(8,128)}, u32[]{:S(2)}) %copy-start.1) | copy-done | bytes 2097176
  113.1 3.4 %last.1 = (f32[2048,256]{1,0:T(8,128)}, f32[128,128]{1,0:T(8,128)}) custom-call(f32[2048,256]{1,0:T(8,128)S(1)} %copy-done.1, f32[16,128,128]{2,1,0:T(8,128)S(1)} %all-to-all-done.rows, f32[16,136,128]{2,1,0:T(8,128)S(1)} %all-to-all-done.3.found, f32[128,128]{1,0:T(8,128)S(1)} %copy-done.2, f32[128,128]{1,0:T(8,128)S(1)} %get-tuple-element.8.wmat, ...), custom_call_target="tpu_custom_call" | custom-call | flops 805306368 | bytes 6291456 | tf_op jit(solution)/shard_map/last/pallas_call | solution.py:232
  (34 shorter events, 3.6 us)
Async XLA Ops:
  0.6 2.0 %copy-start.2 = (f32[128,128]{1,0:T(8,128)S(1)}, f32[128,128]{1,0:T(8,128)}, u32[]{:S(2)}) copy-start(f32[128,128]{1,0:T(8,128)} %panel.3) | copy-start | bytes 196612
  2.6 19.1 %collective-permute-start.3 = (f32[128,128]{1,0:T(8,128)S(1)}, f32[128,128]{1,0:T(8,128)S(1)}, u32[]{:S(2)}, u32[]{:S(2)}) collective-permute-start(f32[128,128]{1,0:T(8,128)S(1)} %copy-done.2), channel_id=1, source_target_pairs={{256,0},{257,16},{258,1},{259,17},{260,2},{261,18},{262,3},{263,19... | collective-permute-start | bytes 196616 | tf_op jit(solution)/shard_map/ppermute | solution.py:53
  3.9 17.8 %collective-permute-start.2 = (f32[128,128]{1,0:T(8,128)S(1)}, f32[128,128]{1,0:T(8,128)S(1)}, u32[]{:S(2)}, u32[]{:S(2)}) collective-permute-start(f32[128,128]{1,0:T(8,128)S(1)} %copy-done.2), channel_id=1, source_target_pairs={{256,128},{257,144},{258,129},{259,145},{260,130},{261,146},{262,1... | collective-permute-start | bytes 196616 | tf_op jit(solution)/shard_map/ppermute | solution.py:53
  4.6 17.1 %collective-permute-start.1 = (f32[128,128]{1,0:T(8,128)S(1)}, f32[128,128]{1,0:T(8,128)S(1)}, u32[]{:S(2)}, u32[]{:S(2)}) collective-permute-start(f32[128,128]{1,0:T(8,128)S(1)} %copy-done.2), channel_id=1, source_target_pairs={{256,384},{257,400},{258,385},{259,401},{260,386},{261,402},{262,3... | collective-permute-start | bytes 196616 | tf_op jit(solution)/shard_map/ppermute | solution.py:53
  5.2 16.4 %collective-permute-start = (f32[128,128]{1,0:T(8,128)S(1)}, f32[128,128]{1,0:T(8,128)S(1)}, u32[]{:S(2)}, u32[]{:S(2)}) collective-permute-start(f32[128,128]{1,0:T(8,128)S(1)} %copy-done.2), channel_id=1, source_target_pairs={{256,256},{257,272},{258,257},{259,273},{260,258},{261,274},{262,2... | collective-permute-start | bytes 196616 | tf_op jit(solution)/shard_map/ppermute | solution.py:53
  5.9 30.6 %all-to-all-start = ((f32[16,128,128]{2,1,0:T(8,128)}), f32[16,128,128]{2,1,0:T(8,128)S(1)}, u32[]{:S(2)}, u32[]{:S(2)}) async-start(f32[16,128,128]{2,1,0:T(8,128)} %broadcast_in_dim.12), calls=%async_computation | async-start | bytes 2097152 | tf_op jit(solution)/shard_map/all_to_all | solution.py:256
  21.7 2.6 %collective-permute-start.4 = (f32[128,128]{1,0:T(8,128)S(1)}, f32[128,128]{1,0:T(8,128)S(1)}, u32[]{:S(2)}, u32[]{:S(2)}) collective-permute-start(f32[128,128]{1,0:T(8,128)S(1)} %add_add_fusion.1), channel_id=1, source_target_pairs={{0,64},{128,192},{256,320},{384,448},{1,65},{129,193},{257,321},{3... | collective-permute-start | bytes 196616 | tf_op jit(solution)/shard_map/ppermute | solution.py:75
  24.3 3.0 %collective-permute-start.5 = (f32[128,128]{1,0:T(8,128)S(1)}, f32[128,128]{1,0:T(8,128)S(1)}, u32[]{:S(2)}, u32[]{:S(2)}) collective-permute-start(f32[128,128]{1,0:T(8,128)S(1)} %add.36), channel_id=1, source_target_pairs={{0,32},{64,96},{128,160},{192,224},{256,288},{320,352},{384,416},{... | collective-permute-start | bytes 196616 | tf_op jit(solution)/shard_map/ppermute | solution.py:75
  27.3 6.6 %collective-permute-start.6 = (f32[128,128]{1,0:T(8,128)S(1)}, f32[128,128]{1,0:T(8,128)S(1)}, u32[]{:S(2)}, u32[]{:S(2)}) collective-permute-start(f32[128,128]{1,0:T(8,128)S(1)} %add.37.mine), channel_id=1, source_target_pairs={{0,16},{16,0},{1,17},{17,1},{2,18},{18,2},{3,19},{19,3},{4,20},{20... | collective-permute-start | bytes 196616 | tf_op jit(solution)/shard_map/ppermute | solution.py:81
  33.9 1.6 %copy-start = (f32[2048,256]{1,0:T(8,128)S(1)}, f32[2048,256]{1,0:T(8,128)}, u32[]{:S(2)}) copy-start(f32[2048,256]{1,0:T(8,128)} %slab.3) | copy-start | bytes 6291460
  35.5 1.0 copy-start.4
  37.2 23.5 %copy-start.3 = (f32[128,128]{1,0:T(8,128)S(1)}, f32[128,128]{1,0:T(8,128)}, u32[]{:S(2)}) copy-start(f32[128,128]{1,0:T(8,128)} %tfactor.3) | copy-start | bytes 196612
  60.9 24.8 %collective-permute-start.10 = (f32[128,128]{1,0:T(8,128)S(1)}, f32[128,128]{1,0:T(8,128)S(1)}, u32[]{:S(2)}, u32[]{:S(2)}) collective-permute-start(f32[128,128]{1,0:T(8,128)S(1)} %get-tuple-element.8.wmat), channel_id=1, source_target_pairs={{256,0},{257,16},{258,1},{259,17},{260,2},{261,18},{262,3},{263,19... | collective-permute-start | bytes 196616 | tf_op jit(solution)/shard_map/ppermute | solution.py:53
  62.2 23.6 %collective-permute-start.9 = (f32[128,128]{1,0:T(8,128)S(1)}, f32[128,128]{1,0:T(8,128)S(1)}, u32[]{:S(2)}, u32[]{:S(2)}) collective-permute-start(f32[128,128]{1,0:T(8,128)S(1)} %get-tuple-element.8.wmat), channel_id=1, source_target_pairs={{256,128},{257,144},{258,129},{259,145},{260,130},{261,146},{262,1... | collective-permute-start | bytes 196616 | tf_op jit(solution)/shard_map/ppermute | solution.py:53
  62.9 22.9 %collective-permute-start.8 = (f32[128,128]{1,0:T(8,128)S(1)}, f32[128,128]{1,0:T(8,128)S(1)}, u32[]{:S(2)}, u32[]{:S(2)}) collective-permute-start(f32[128,128]{1,0:T(8,128)S(1)} %get-tuple-element.8.wmat), channel_id=1, source_target_pairs={{256,384},{257,400},{258,385},{259,401},{260,386},{261,402},{262,3... | collective-permute-start | bytes 196616 | tf_op jit(solution)/shard_map/ppermute | solution.py:53
  63.6 4.5 %collective-permute-start.7 = (f32[8,128]{1,0:T(8,128)S(1)}, f32[8,128]{1,0:T(8,128)S(1)}, u32[]{:S(2)}, u32[]{:S(2)}) collective-permute-start(f32[8,128]{1,0:T(8,128)S(1)} %get-tuple-element.9), channel_id=1, source_target_pairs={{0,16},{16,0},{1,17},{17,1},{2,18},{18,2},{3,19},{19,3},{4,20},{20... | collective-permute-start | bytes 12296 | tf_op jit(solution)/shard_map/ppermute | solution.py:81
  68.7 20.5 %all-to-all-start.2 = ((f32[16,8,128]{2,1,0:T(8,128)}), f32[16,8,128]{2,1,0:T(8,128)S(1)}, u32[]{:S(2)}, u32[]{:S(2)}) async-start(f32[16,8,128]{2,1,0:T(8,128)} %broadcast_in_dim.14), calls=%async_computation.2 | async-start | bytes 131072 | tf_op jit(solution)/shard_map/all_to_all | solution.py:265
  85.1 9.8 %collective-permute-start.11 = (f32[128,128]{1,0:T(8,128)S(1)}, f32[128,128]{1,0:T(8,128)S(1)}, u32[]{:S(2)}, u32[]{:S(2)}) collective-permute-start(f32[128,128]{1,0:T(8,128)S(1)} %get-tuple-element.8.wmat), channel_id=1, source_target_pairs={{256,256},{257,272},{258,257},{259,273},{260,258},{261,274},{262,2... | collective-permute-start | bytes 196616 | tf_op jit(solution)/shard_map/ppermute | solution.py:53
  90.3 21.2 %all-to-all-start.3 = ((f32[16,136,128]{2,1,0:T(8,128)}), f32[16,136,128]{2,1,0:T(8,128)S(1)}, u32[]{:S(2)}, u32[]{:S(2)}) async-start(f32[16,136,128]{2,1,0:T(8,128)} %broadcast_in_dim.15), calls=%async_computation.3 | async-start | bytes 2228224 | tf_op jit(solution)/shard_map/all_to_all | solution.py:43
  95.0 4.6 %collective-permute-start.12 = (f32[128,128]{1,0:T(8,128)S(1)}, f32[128,128]{1,0:T(8,128)S(1)}, u32[]{:S(2)}, u32[]{:S(2)}) collective-permute-start(f32[128,128]{1,0:T(8,128)S(1)} %add.41), channel_id=1, source_target_pairs={{0,64},{128,192},{256,320},{384,448},{1,65},{129,193},{257,321},{3... | collective-permute-start | bytes 196616 | tf_op jit(solution)/shard_map/ppermute | solution.py:75
  99.6 2.8 %collective-permute-start.13 = (f32[128,128]{1,0:T(8,128)S(1)}, f32[128,128]{1,0:T(8,128)S(1)}, u32[]{:S(2)}, u32[]{:S(2)}) collective-permute-start(f32[128,128]{1,0:T(8,128)S(1)} %add.42), channel_id=1, source_target_pairs={{0,32},{64,96},{128,160},{192,224},{256,288},{320,352},{384,416},{... | collective-permute-start | bytes 196616 | tf_op jit(solution)/shard_map/ppermute | solution.py:75
  102.4 6.1 %collective-permute-start.14 = (f32[128,128]{1,0:T(8,128)S(1)}, f32[128,128]{1,0:T(8,128)S(1)}, u32[]{:S(2)}, u32[]{:S(2)}) collective-permute-start(f32[128,128]{1,0:T(8,128)S(1)} %add.43.wmine), channel_id=1, source_target_pairs={{0,16},{16,0},{1,17},{17,1},{2,18},{18,2},{3,19},{19,3},{4,20},{20... | collective-permute-start | bytes 196616 | tf_op jit(solution)/shard_map/ppermute | solution.py:81
  111.5 1.6 %copy-start.1 = (f32[2048,256]{1,0:T(8,128)S(1)}, f32[2048,256]{1,0:T(8,128)}, u32[]{:S(2)}) copy-start(f32[2048,256]{1,0:T(8,128)} %slab.3) | copy-start | bytes 6291460

commit v4 on v3

--- a/solution.py
+++ b/solution.py
@@ -10,7 +10,8 @@
 ALL = ROW + COL
 SLICE = 8
 VMEM = 16 << 20
-PARTS = 4
+LAST_VMEM = 50 << 20
+PARTS = 2
 F32 = jnp.float32
 NN = ((1,), (0,))
 NT = ((1,), (1,))
@@ -162,6 +163,25 @@
     )(terms, other_av, tfactor)
 
 
+def spread_kernel(part, other, out):
+    total = part[...] + other[...]
+    for i in range(out.shape[0]):
+        out[i] = total
+
+
+def spread_sum(part, other):
+    vmem = pl.BlockSpec(memory_space=pltpu.VMEM)
+    return pl.pallas_call(
+        spread_kernel,
+        out_shape=jax.ShapeDtypeStruct((lax.axis_size("z"),) + part.shape, F32),
+        in_specs=[vmem] * 2,
+        out_specs=vmem,
+        compiler_params=pltpu.CompilerParams(vmem_limit_bytes=VMEM),
+        cost_estimate=pl.CostEstimate(flops=1*10**9, bytes_accessed=128 * part.size, transcendentals=0),
+        name="spread",
+    )(part, other)
+
+
 def relayed_kernel(got, out):
     out[...] = got[...]
 
@@ -200,9 +220,15 @@
 
 
 def last_kernel(
-    slab, rows, found, panel, wmat, tfactor, pair, updated, correction, result, sems
+    slab, rows, found, panel, wmat, tfactor, pair, updated, correction, result, loads, sems
 ):
     ncol, block, nb = rows.shape
+    size = slab.shape[0] // PARTS
+    copies = []
+    for i in range(PARTS):
+        here = pl.ds(i * size, size)
+        copies.append(pltpu.make_async_copy(slab.at[here, :], result.at[here, :], loads.at[i]))
+        copies[-1].start()
     factor = split(tfactor[...])
     inner = product(split(found[:, block:, :].reshape(nb, nb)), factor, NN)
     middle = product(factor, split(inner), TN)
@@ -211,7 +237,6 @@
     columns_v = right[:, nb:]
     turned = right[:, :nb] - product(split(columns_v), split(both), NN)
     right = split(jnp.concatenate([turned, columns_v], axis=1))
-    size = slab.shape[0] // PARTS
     step = ncol // PARTS
     stores = []
     for i in range(PARTS):
@@ -219,7 +244,9 @@
         left = jnp.concatenate(
             [rows[part].reshape(size, nb), found[part, :block, :].reshape(size, nb)], axis=1
         )
-        result[here, :] = slab[here, :] - product(split(left), right, NT)
+        change = product(split(left), right, NT)
+        copies[i].wait()
+        result[here, :] = result[here, :] - change
         stores.append(pltpu.make_async_copy(result.at[here, :], updated.at[here, :], sems.at[i]))
         stores[-1].start()
     correction[...] = wmat[...] - 0.5 * product(split(panel[...]), split(middle), NN)
@@ -235,10 +262,10 @@
             jax.ShapeDtypeStruct(slab.shape, F32),
             jax.ShapeDtypeStruct(wmat.shape, F32),
         ),
-        in_specs=[vmem] * 7,
+        in_specs=[pl.BlockSpec(memory_space=pl.ANY)] + [vmem] * 6,
         out_specs=(pl.BlockSpec(memory_space=pl.ANY), vmem),
-        scratch_shapes=[pltpu.VMEM(slab.shape, F32), pltpu.SemaphoreType.DMA((PARTS,))],
-        compiler_params=pltpu.CompilerParams(vmem_limit_bytes=VMEM),
+        scratch_shapes=[pltpu.VMEM(slab.shape, F32)] + [pltpu.SemaphoreType.DMA((PARTS,))] * 2,
+        compiler_params=pltpu.CompilerParams(vmem_limit_bytes=LAST_VMEM),
         cost_estimate=pl.CostEstimate(
             flops=12 * slab.size * wmat.shape[1],
             bytes_accessed=4 * (2 * slab.size + 2 * rows.size),
@@ -259,11 +286,11 @@
     other = swapped(mine)
     sent = first(core, slab, rows, panel, other_av, mine, other)
     wmat, part = summed(lax.all_to_all(sent, COL, 0, 0), other_av, tfactor)
-    part = part + swapped(part)
+    other_part = swapped(part)
     early = relayed(sum(place(wmat, (12, 4, 0))))
     held = early + place(wmat, (8,))[0]
     part = lax.all_to_all(
-        copies(part, "z"), "z", 0, 0, axis_index_groups=[[(i + 8) % 16 for i in range(16)]]
+        spread_sum(part, other_part), "z", 0, 0, axis_index_groups=[[(i + 8) % 16 for i in range(16)]]
     ).sum(axis=0)
     found = to_all(jnp.concatenate([wmat, part], axis=0), COL)
     wmine = send_near(held)

time: 117 us -> 116 us (level)
  local copies, waits for them, and re-layouts: 6.87 us -> 4.64 us
  Pallas kernels: 5.23 us -> 7.13 us
    unnamed x10 -> x8, local copies, waits for them, and re-layouts: 3.2 us -> 1.6 us
    pallas_call x1, Pallas kernels: 3.36 us -> 4.62 us  [last(): pl.pallas_call(last_kernel, out_shape=(jax.ShapeDtypeStruct(slab.shape, F...]
    broadcast_in_dim x3 -> x2, local copies, waits for them, and re-layouts: 3.68 us -> 3.04 us  [copies(): return jnp.broadcast_to(value, (lax.axis_size(axis),) + value.shape)]
  transfers between devices with their start and end apart: 18 -> 18, of which waited for: 10 -> 9; matrix products, arithmetic and copies ran while one was open for 2% -> 1% of each run, Pallas kernels for 1% -> 1%
where the time goes in v4:
time: 116 us; the launch traced here: 115 us
  starting transfers between devices  56.3 us (49%)
  blocking collectives  23.5 us (20%)
  waiting for transfers between devices  22.3 us (19%)
  Pallas kernels  7.13 us (6%)
  local copies, waits for them, and re-layouts  4.64 us (4%)
    all_to_all x1, blocking collectives, on_device(): wmat, part = summed(lax.all_to_all(sent, COL, 0, 0), other_av, tfactor)  23.5 us
    all_to_all x1, starting transfers between devices, on_device(): lax.all_to_all(spread_sum(part, other_part), 'z', 0, 0, axis_index_groups...  16.4 us
    ppermute x3, starting transfers between devices, swapped(): return lax.ppermute(held, 'core', [(0, 1), (1, 0)])  14.7 us
    ppermute x8, waiting for transfers between devices, place(): lax.ppermute(value, ALL, [(index(nz // 2, k, c), index(target, c % 2, (k...  8.18 us
    all_to_all x1, starting transfers between devices, on_device(): rows = lax.all_to_all(spread, COL, 0, 0)  7.6 us
    ppermute x4, starting transfers between devices, send_near(): lax.ppermute(held, 'z', [(z, z + step) for z in range(0, nz, 2 * step)])  7.02 us
    ppermute x8, starting transfers between devices, place(): lax.ppermute(value, ALL, [(index(nz // 2, k, c), index(target, c % 2, (k...  6.55 us
    ppermute x4, waiting for transfers between devices, send_near(): lax.ppermute(held, 'z', [(z, z + step) for z in range(0, nz, 2 * step)])  5.94 us
  transfers between devices with their start and end apart: 18, of which 9 were waited for; matrix products, arithmetic and copies ran while one was open for 1% of the time, Pallas kernels for 1%

profile of v4, /device:TPU:1, one launch (start us, length us, event | category | flops | bytes accessed | tf_op | source)
XLA Modules:
  0.0 114.9 jit_solution(13048650520354941508)
XLA Ops:
  0.6 2.0 %broadcast_in_dim.9 = f32[16,128,128]{2,1,0:T(8,128)} broadcast(f32[128,128]{1,0:T(8,128)} %panel.3), dimensions={1,2} | broadcast | bytes 1114112 | tf_op jit(solution)/shard_map/broadcast_in_dim | solution.py:40
  2.6 1.3 %collective-permute-start.3 = (f32[128,128]{1,0:T(8,128)S(1)}, f32[128,128]{1,0:T(8,128)S(1)}, u32[]{:S(2)}, u32[]{:S(2)}) collective-permute-start(f32[128,128]{1,0:T(8,128)S(1)} %copy-done.1), channel_id=1, source_target_pairs={{256,0},{257,16},{258,1},{259,17},{260,2},{261,18},{262,3},{263,19... | collective-permute-start | bytes 196616 | tf_op jit(solution)/shard_map/ppermute | solution.py:54
  3.9 0.7 collective-permute-start.2
  4.6 0.7 collective-permute-start.1
  5.2 0.7 collective-permute-start
  5.9 7.6 %all-to-all-start = ((f32[16,128,128]{2,1,0:T(8,128)}), f32[16,128,128]{2,1,0:T(8,128)S(1)}, u32[]{:S(2)}, u32[]{:S(2)}) async-start(f32[16,128,128]{2,1,0:T(8,128)} %broadcast_in_dim.9), calls=%async_computation | async-start | bytes 2097152 | tf_op jit(solution)/shard_map/all_to_all | solution.py:283
  13.5 8.2 %collective-permute-done.3 = f32[128,128]{1,0:T(8,128)S(1)} collective-permute-done((f32[128,128]{1,0:T(8,128)S(1)}, f32[128,128]{1,0:T(8,128)S(1)}, u32[]{:S(2)}, u32[]{:S(2)}) %collective-permute-start.3) | collective-permute-done | bytes 65568 | tf_op jit(solution)/shard_map/ppermute | solution.py:54
  21.7 1.3 %collective-permute-start.4 = (f32[128,128]{1,0:T(8,128)S(1)}, f32[128,128]{1,0:T(8,128)S(1)}, u32[]{:S(2)}, u32[]{:S(2)}) collective-permute-start(f32[128,128]{1,0:T(8,128)S(1)} %add_add_fusion.1), channel_id=1, source_target_pairs={{0,64},{128,192},{256,320},{384,448},{1,65},{129,193},{257,321},{3... | collective-permute-start | bytes 196616 | tf_op jit(solution)/shard_map/ppermute | solution.py:76
  23.0 1.3 %collective-permute-done.4 = f32[128,128]{1,0:T(8,128)S(1)} collective-permute-done((f32[128,128]{1,0:T(8,128)S(1)}, f32[128,128]{1,0:T(8,128)S(1)}, u32[]{:S(2)}, u32[]{:S(2)}) %collective-permute-start.4) | collective-permute-done | bytes 65568 | tf_op jit(solution)/shard_map/ppermute | solution.py:76
  24.3 1.3 %collective-permute-start.5 = (f32[128,128]{1,0:T(8,128)S(1)}, f32[128,128]{1,0:T(8,128)S(1)}, u32[]{:S(2)}, u32[]{:S(2)}) collective-permute-start(f32[128,128]{1,0:T(8,128)S(1)} %add.33), channel_id=1, source_target_pairs={{0,32},{64,96},{128,160},{192,224},{256,288},{320,352},{384,416},{... | collective-permute-start | bytes 196616 | tf_op jit(solution)/shard_map/ppermute | solution.py:76
  25.6 1.7 %collective-permute-done.5 = f32[128,128]{1,0:T(8,128)S(1)} collective-permute-done((f32[128,128]{1,0:T(8,128)S(1)}, f32[128,128]{1,0:T(8,128)S(1)}, u32[]{:S(2)}, u32[]{:S(2)}) %collective-permute-start.5) | collective-permute-done | bytes 65568 | tf_op jit(solution)/shard_map/ppermute | solution.py:76
  27.3 5.7 %collective-permute-start.6 = (f32[128,128]{1,0:T(8,128)S(1)}, f32[128,128]{1,0:T(8,128)S(1)}, u32[]{:S(2)}, u32[]{:S(2)}) collective-permute-start(f32[128,128]{1,0:T(8,128)S(1)} %add.34.mine), channel_id=1, source_target_pairs={{0,16},{16,0},{1,17},{17,1},{2,18},{18,2},{3,19},{19,3},{4,20},{20... | collective-permute-start | bytes 196616 | tf_op jit(solution)/shard_map/ppermute | solution.py:82
  33.1 0.9 collective-permute-done.6.other
  33.9 1.6 %copy-done = f32[2048,256]{1,0:T(8,128)S(1)} copy-done((f32[2048,256]{1,0:T(8,128)S(1)}, f32[2048,256]{1,0:T(8,128)}, u32[]{:S(2)}) %copy-start) | copy-done | bytes 2097176
  35.5 1.0 first.1.terms
  37.2 23.5 %all_to_all.20.terms = f32[16,136,128]{2,1,0:T(8,128)S(1)} all-to-all(f32[16,136,128]{2,1,0:T(8,128)S(1)} %cross.1), channel_id=1, replica_groups=mesh['z'=16,'core'=2,'y'=4,'x'=4] {'y','x'}, dimensions={0} | all-to-all | bytes 2228224 | tf_op jit(solution)/shard_map/all_to_all | solution.py:288
  60.9 3.7 %collective-permute-start.7 = (f32[8,128]{1,0:T(8,128)S(1)}, f32[8,128]{1,0:T(8,128)S(1)}, u32[]{:S(2)}, u32[]{:S(2)}) collective-permute-start(f32[8,128]{1,0:T(8,128)S(1)} %get-tuple-element.9.part), channel_id=1, source_target_pairs={{0,16},{16,0},{1,17},{17,1},{2,18},{18,2},{3,19},{19,3},{4,20},{20... | collective-permute-start | bytes 12296 | tf_op jit(solution)/shard_map/ppermute | solution.py:82
  64.6 1.3 %collective-permute-start.10 = (f32[128,128]{1,0:T(8,128)S(1)}, f32[128,128]{1,0:T(8,128)S(1)}, u32[]{:S(2)}, u32[]{:S(2)}) collective-permute-start(f32[128,128]{1,0:T(8,128)S(1)} %get-tuple-element.8.wmat), channel_id=1, source_target_pairs={{256,0},{257,16},{258,1},{259,17},{260,2},{261,18},{262,3},{263,19... | collective-permute-start | bytes 196616 | tf_op jit(solution)/shard_map/ppermute | solution.py:54
  65.9 0.7 collective-permute-start.9
  66.6 0.7 collective-permute-start.8
  67.9 16.4 %all-to-all-start.2 = ((f32[16,8,128]{2,1,0:T(8,128)}), f32[16,8,128]{2,1,0:T(8,128)S(1)}, u32[]{:S(2)}, u32[]{:S(2)}) async-start(f32[16,8,128]{2,1,0:T(8,128)} %spread.1), calls=%async_computation.2 | async-start | bytes 131072 | tf_op jit(solution)/shard_map/all_to_all | solution.py:292
  85.0 3.6 %all-to-all-done.2 = f32[16,8,128]{2,1,0:T(8,128)S(1)} async-done(((f32[16,8,128]{2,1,0:T(8,128)}), f32[16,8,128]{2,1,0:T(8,128)S(1)}, u32[]{:S(2)}, u32[]{:S(2)}) %all-to-all-start.2) | async-done | bytes 65568 | tf_op jit(solution)/shard_map/all_to_all | solution.py:292
  88.7 1.1 broadcast_in_dim.11
  89.7 4.0 %all-to-all-start.3 = ((f32[16,136,128]{2,1,0:T(8,128)}), f32[16,136,128]{2,1,0:T(8,128)S(1)}, u32[]{:S(2)}, u32[]{:S(2)}) async-start(f32[16,136,128]{2,1,0:T(8,128)} %broadcast_in_dim.11), calls=%async_computation.3 | async-start | bytes 2228224 | tf_op jit(solution)/shard_map/all_to_all | solution.py:44
  93.8 3.1 %collective-permute-start.12 = (f32[128,128]{1,0:T(8,128)S(1)}, f32[128,128]{1,0:T(8,128)S(1)}, u32[]{:S(2)}, u32[]{:S(2)}) collective-permute-start(f32[128,128]{1,0:T(8,128)S(1)} %add.37), channel_id=1, source_target_pairs={{0,64},{128,192},{256,320},{384,448},{1,65},{129,193},{257,321},{3... | collective-permute-start | bytes 196616 | tf_op jit(solution)/shard_map/ppermute | solution.py:76
  97.0 1.3 %collective-permute-done.12 = f32[128,128]{1,0:T(8,128)S(1)} collective-permute-done((f32[128,128]{1,0:T(8,128)S(1)}, f32[128,128]{1,0:T(8,128)S(1)}, u32[]{:S(2)}, u32[]{:S(2)}) %collective-permute-start.12) | collective-permute-done | bytes 65568 | tf_op jit(solution)/shard_map/ppermute | solution.py:76
  98.3 1.3 %collective-permute-start.13 = (f32[128,128]{1,0:T(8,128)S(1)}, f32[128,128]{1,0:T(8,128)S(1)}, u32[]{:S(2)}, u32[]{:S(2)}) collective-permute-start(f32[128,128]{1,0:T(8,128)S(1)} %add.38), channel_id=1, source_target_pairs={{0,32},{64,96},{128,160},{192,224},{256,288},{320,352},{384,416},{... | collective-permute-start | bytes 196616 | tf_op jit(solution)/shard_map/ppermute | solution.py:76
  99.6 1.7 %collective-permute-done.13 = f32[128,128]{1,0:T(8,128)S(1)} collective-permute-done((f32[128,128]{1,0:T(8,128)S(1)}, f32[128,128]{1,0:T(8,128)S(1)}, u32[]{:S(2)}, u32[]{:S(2)}) %collective-permute-start.13) | collective-permute-done | bytes 65568 | tf_op jit(solution)/shard_map/ppermute | solution.py:76
  101.3 5.3 %collective-permute-start.14 = (f32[128,128]{1,0:T(8,128)S(1)}, f32[128,128]{1,0:T(8,128)S(1)}, u32[]{:S(2)}, u32[]{:S(2)}) collective-permute-start(f32[128,128]{1,0:T(8,128)S(1)} %add.39.wmine), channel_id=1, source_target_pairs={{0,16},{16,0},{1,17},{17,1},{2,18},{18,2},{3,19},{19,3},{4,20},{20... | collective-permute-start | bytes 196616 | tf_op jit(solution)/shard_map/ppermute | solution.py:82
  106.5 0.9 collective-permute-done.14.wother
  107.4 2.9 %all-to-all-done.3.found = f32[16,136,128]{2,1,0:T(8,128)S(1)} async-done(((f32[16,136,128]{2,1,0:T(8,128)}), f32[16,136,128]{2,1,0:T(8,128)S(1)}, u32[]{:S(2)}, u32[]{:S(2)}) %all-to-all-start.3) | async-done | bytes 1114144 | tf_op jit(solution)/shard_map/all_to_all | solution.py:44
  110.3 4.6 %last.1 = (f32[2048,256]{1,0:T(8,128)}, f32[128,128]{1,0:T(8,128)}) custom-call(f32[2048,256]{1,0:T(8,128)} %slab.3, f32[16,128,128]{2,1,0:T(8,128)S(1)} %all-to-all-done.rows, f32[16,136,128]{2,1,0:T(8,128)S(1)} %all-to-all-done.3.found, f32[128,128]{1,0:T(8,128)S(1)} %copy-done.1, f32[128,128]{1,0:T(8,128)S(1)} %get-tuple-element.8.wmat, ...), custom_call_target="tpu_custom_call" | custom-call | flops 805306368 | bytes 6291456 | tf_op jit(solution)/shard_map/last/pallas_call | solution.py:259
  (31 shorter events, 2.3 us)
Async XLA Ops:
  0.6 2.0 %copy-start.1 = (f32[128,128]{1,0:T(8,128)S(1)}, f32[128,128]{1,0:T(8,128)}, u32[]{:S(2)}) copy-start(f32[128,128]{1,0:T(8,128)} %panel.3) | copy-start | bytes 196612
  2.6 19.1 %collective-permute-start.3 = (f32[128,128]{1,0:T(8,128)S(1)}, f32[128,128]{1,0:T(8,128)S(1)}, u32[]{:S(2)}, u32[]{:S(2)}) collective-permute-start(f32[128,128]{1,0:T(8,128)S(1)} %copy-done.1), channel_id=1, source_target_pairs={{256,0},{257,16},{258,1},{259,17},{260,2},{261,18},{262,3},{263,19... | collective-permute-start | bytes 196616 | tf_op jit(solution)/shard_map/ppermute | solution.py:54
  3.9 17.8 %collective-permute-start.2 = (f32[128,128]{1,0:T(8,128)S(1)}, f32[128,128]{1,0:T(8,128)S(1)}, u32[]{:S(2)}, u32[]{:S(2)}) collective-permute-start(f32[128,128]{1,0:T(8,128)S(1)} %copy-done.1), channel_id=1, source_target_pairs={{256,128},{257,144},{258,129},{259,145},{260,130},{261,146},{262,1... | collective-permute-start | bytes 196616 | tf_op jit(solution)/shard_map/ppermute | solution.py:54
  4.6 17.1 %collective-permute-start.1 = (f32[128,128]{1,0:T(8,128)S(1)}, f32[128,128]{1,0:T(8,128)S(1)}, u32[]{:S(2)}, u32[]{:S(2)}) collective-permute-start(f32[128,128]{1,0:T(8,128)S(1)} %copy-done.1), channel_id=1, source_target_pairs={{256,384},{257,400},{258,385},{259,401},{260,386},{261,402},{262,3... | collective-permute-start | bytes 196616 | tf_op jit(solution)/shard_map/ppermute | solution.py:54
  5.2 16.4 %collective-permute-start = (f32[128,128]{1,0:T(8,128)S(1)}, f32[128,128]{1,0:T(8,128)S(1)}, u32[]{:S(2)}, u32[]{:S(2)}) collective-permute-start(f32[128,128]{1,0:T(8,128)S(1)} %copy-done.1), channel_id=1, source_target_pairs={{256,256},{257,272},{258,257},{259,273},{260,258},{261,274},{262,2... | collective-permute-start | bytes 196616 | tf_op jit(solution)/shard_map/ppermute | solution.py:54
  5.9 30.6 %all-to-all-start = ((f32[16,128,128]{2,1,0:T(8,128)}), f32[16,128,128]{2,1,0:T(8,128)S(1)}, u32[]{:S(2)}, u32[]{:S(2)}) async-start(f32[16,128,128]{2,1,0:T(8,128)} %broadcast_in_dim.9), calls=%async_computation | async-start | bytes 2097152 | tf_op jit(solution)/shard_map/all_to_all | solution.py:283
  21.7 2.6 %collective-permute-start.4 = (f32[128,128]{1,0:T(8,128)S(1)}, f32[128,128]{1,0:T(8,128)S(1)}, u32[]{:S(2)}, u32[]{:S(2)}) collective-permute-start(f32[128,128]{1,0:T(8,128)S(1)} %add_add_fusion.1), channel_id=1, source_target_pairs={{0,64},{128,192},{256,320},{384,448},{1,65},{129,193},{257,321},{3... | collective-permute-start | bytes 196616 | tf_op jit(solution)/shard_map/ppermute | solution.py:76
  24.3 3.0 %collective-permute-start.5 = (f32[128,128]{1,0:T(8,128)S(1)}, f32[128,128]{1,0:T(8,128)S(1)}, u32[]{:S(2)}, u32[]{:S(2)}) collective-permute-start(f32[128,128]{1,0:T(8,128)S(1)} %add.33), channel_id=1, source_target_pairs={{0,32},{64,96},{128,160},{192,224},{256,288},{320,352},{384,416},{... | collective-permute-start | bytes 196616 | tf_op jit(solution)/shard_map/ppermute | solution.py:76
  27.3 6.6 %collective-permute-start.6 = (f32[128,128]{1,0:T(8,128)S(1)}, f32[128,128]{1,0:T(8,128)S(1)}, u32[]{:S(2)}, u32[]{:S(2)}) collective-permute-start(f32[128,128]{1,0:T(8,128)S(1)} %add.34.mine), channel_id=1, source_target_pairs={{0,16},{16,0},{1,17},{17,1},{2,18},{18,2},{3,19},{19,3},{4,20},{20... | collective-permute-start | bytes 196616 | tf_op jit(solution)/shard_map/ppermute | solution.py:82
  33.9 1.6 %copy-start = (f32[2048,256]{1,0:T(8,128)S(1)}, f32[2048,256]{1,0:T(8,128)}, u32[]{:S(2)}) copy-start(f32[2048,256]{1,0:T(8,128)} %slab.3) | copy-start | bytes 6291460
  35.5 1.0 copy-start.3
  37.2 23.5 %copy-start.2 = (f32[128,128]{1,0:T(8,128)S(1)}, f32[128,128]{1,0:T(8,128)}, u32[]{:S(2)}) copy-start(f32[128,128]{1,0:T(8,128)} %tfactor.3) | copy-start | bytes 196612
  60.9 6.3 %collective-permute-start.7 = (f32[8,128]{1,0:T(8,128)S(1)}, f32[8,128]{1,0:T(8,128)S(1)}, u32[]{:S(2)}, u32[]{:S(2)}) collective-permute-start(f32[8,128]{1,0:T(8,128)S(1)} %get-tuple-element.9.part), channel_id=1, source_target_pairs={{0,16},{16,0},{1,17},{17,1},{2,18},{18,2},{3,19},{19,3},{4,20},{20... | collective-permute-start | bytes 12296 | tf_op jit(solution)/shard_map/ppermute | solution.py:82
  64.6 20.4 %collective-permute-start.10 = (f32[128,128]{1,0:T(8,128)S(1)}, f32[128,128]{1,0:T(8,128)S(1)}, u32[]{:S(2)}, u32[]{:S(2)}) collective-permute-start(f32[128,128]{1,0:T(8,128)S(1)} %get-tuple-element.8.wmat), channel_id=1, source_target_pairs={{256,0},{257,16},{258,1},{259,17},{260,2},{261,18},{262,3},{263,19... | collective-permute-start | bytes 196616 | tf_op jit(solution)/shard_map/ppermute | solution.py:54
  65.9 19.1 %collective-permute-start.9 = (f32[128,128]{1,0:T(8,128)S(1)}, f32[128,128]{1,0:T(8,128)S(1)}, u32[]{:S(2)}, u32[]{:S(2)}) collective-permute-start(f32[128,128]{1,0:T(8,128)S(1)} %get-tuple-element.8.wmat), channel_id=1, source_target_pairs={{256,128},{257,144},{258,129},{259,145},{260,130},{261,146},{262,1... | collective-permute-start | bytes 196616 | tf_op jit(solution)/shard_map/ppermute | solution.py:54
  66.6 18.4 %collective-permute-start.8 = (f32[128,128]{1,0:T(8,128)S(1)}, f32[128,128]{1,0:T(8,128)S(1)}, u32[]{:S(2)}, u32[]{:S(2)}) collective-permute-start(f32[128,128]{1,0:T(8,128)S(1)} %get-tuple-element.8.wmat), channel_id=1, source_target_pairs={{256,384},{257,400},{258,385},{259,401},{260,386},{261,402},{262,3... | collective-permute-start | bytes 196616 | tf_op jit(solution)/shard_map/ppermute | solution.py:54
  67.9 20.7 %all-to-all-start.2 = ((f32[16,8,128]{2,1,0:T(8,128)}), f32[16,8,128]{2,1,0:T(8,128)S(1)}, u32[]{:S(2)}, u32[]{:S(2)}) async-start(f32[16,8,128]{2,1,0:T(8,128)} %spread.1), calls=%async_computation.2 | async-start | bytes 131072 | tf_op jit(solution)/shard_map/all_to_all | solution.py:292
  84.3 9.5 %collective-permute-start.11 = (f32[128,128]{1,0:T(8,128)S(1)}, f32[128,128]{1,0:T(8,128)S(1)}, u32[]{:S(2)}, u32[]{:S(2)}) collective-permute-start(f32[128,128]{1,0:T(8,128)S(1)} %get-tuple-element.8.wmat), channel_id=1, source_target_pairs={{256,256},{257,272},{258,257},{259,273},{260,258},{261,274},{262,2... | collective-permute-start | bytes 196616 | tf_op jit(solution)/shard_map/ppermute | solution.py:54
  89.7 20.6 %all-to-all-start.3 = ((f32[16,136,128]{2,1,0:T(8,128)}), f32[16,136,128]{2,1,0:T(8,128)S(1)}, u32[]{:S(2)}, u32[]{:S(2)}) async-start(f32[16,136,128]{2,1,0:T(8,128)} %broadcast_in_dim.11), calls=%async_computation.3 | async-start | bytes 2228224 | tf_op jit(solution)/shard_map/all_to_all | solution.py:44
  93.8 4.5 %collective-permute-start.12 = (f32[128,128]{1,0:T(8,128)S(1)}, f32[128,128]{1,0:T(8,128)S(1)}, u32[]{:S(2)}, u32[]{:S(2)}) collective-permute-start(f32[128,128]{1,0:T(8,128)S(1)} %add.37), channel_id=1, source_target_pairs={{0,64},{128,192},{256,320},{384,448},{1,65},{129,193},{257,321},{3... | collective-permute-start | bytes 196616 | tf_op jit(solution)/shard_map/ppermute | solution.py:76
  98.3 3.0 %collective-permute-start.13 = (f32[128,128]{1,0:T(8,128)S(1)}, f32[128,128]{1,0:T(8,128)S(1)}, u32[]{:S(2)}, u32[]{:S(2)}) collective-permute-start(f32[128,128]{1,0:T(8,128)S(1)} %add.38), channel_id=1, source_target_pairs={{0,32},{64,96},{128,160},{192,224},{256,288},{320,352},{384,416},{... | collective-permute-start | bytes 196616 | tf_op jit(solution)/shard_map/ppermute | solution.py:76
  101.3 6.1 %collective-permute-start.14 = (f32[128,128]{1,0:T(8,128)S(1)}, f32[128,128]{1,0:T(8,128)S(1)}, u32[]{:S(2)}, u32[]{:S(2)}) collective-permute-start(f32[128,128]{1,0:T(8,128)S(1)} %add.39.wmine), channel_id=1, source_target_pairs={{0,16},{16,0},{1,17},{17,1},{2,18},{18,2},{3,19},{19,3},{4,20},{20... | collective-permute-start | bytes 196616 | tf_op jit(solution)/shard_map/ppermute | solution.py:82

commit v5 on v4

--- a/solution.py
+++ b/solution.py
@@ -281,7 +281,7 @@
     core = lax.axis_index("core").astype(jnp.int32)[None]
     tied, spread = lax.optimization_barrier((panel, copies(panel, COL)))
     rows = lax.all_to_all(spread, COL, 0, 0)
-    held = sum(place(tied, (8, 12, 4, 0)))
+    held = sum(place(tied, (12, 8, 4, 0)))
     mine = send_near(held)
     other = swapped(mine)
     sent = first(core, slab, rows, panel, other_av, mine, other)

time: 116 us -> 116 us (level)
  no operation moved by 1% of the time
where the time goes in v5:
time: 116 us; the launch traced here: 115 us
  starting transfers between devices  56.7 us (49%)
  blocking collectives  23.5 us (20%)
  waiting for transfers between devices  22.2 us (19%)
  Pallas kernels  7.13 us (6%)
  local copies, waits for them, and re-layouts  4.64 us (4%)
    all_to_all x1, blocking collectives, on_device(): wmat, part = summed(lax.all_to_all(sent, COL, 0, 0), other_av, tfactor)  23.5 us
    all_to_all x1, starting transfers between devices, on_device(): lax.all_to_all(spread_sum(part, other_part), 'z', 0, 0, axis_index_groups...  16.9 us
    ppermute x3, starting transfers between devices, swapped(): return lax.ppermute(held, 'core', [(0, 1), (1, 0)])  14.7 us
    ppermute x8, waiting for transfers between devices, place(): lax.ppermute(value, ALL, [(index(nz // 2, k, c), index(target, c % 2, (k...  8.18 us
    all_to_all x1, starting transfers between devices, on_device(): rows = lax.all_to_all(spread, COL, 0, 0)  7.6 us
    ppermute x4, starting transfers between devices, send_near(): lax.ppermute(held, 'z', [(z, z + step) for z in range(0, nz, 2 * step)])  7.03 us
    ppermute x8, starting transfers between devices, place(): lax.ppermute(value, ALL, [(index(nz // 2, k, c), index(target, c % 2, (k...  6.55 us
    ppermute x4, waiting for transfers between devices, send_near(): lax.ppermute(held, 'z', [(z, z + step) for z in range(0, nz, 2 * step)])  5.93 us
  transfers between devices with their start and end apart: 18, of which 9 were waited for; matrix products, arithmetic and copies ran while one was open for 1% of the time, Pallas kernels for 1%

profile of v5, /device:TPU:1, one launch (start us, length us, event | category | flops | bytes accessed | tf_op | source)
XLA Modules:
  0.0 115.2 jit_solution(2242300989196711048)
XLA Ops:
  0.6 2.0 %broadcast_in_dim.9 = f32[16,128,128]{2,1,0:T(8,128)} broadcast(f32[128,128]{1,0:T(8,128)} %panel.3), dimensions={1,2} | broadcast | bytes 1114112 | tf_op jit(solution)/shard_map/broadcast_in_dim | solution.py:40
  2.6 1.3 %collective-permute-start.3 = (f32[128,128]{1,0:T(8,128)S(1)}, f32[128,128]{1,0:T(8,128)S(1)}, u32[]{:S(2)}, u32[]{:S(2)}) collective-permute-start(f32[128,128]{1,0:T(8,128)S(1)} %copy-done.1), channel_id=1, source_target_pairs={{256,0},{257,16},{258,1},{259,17},{260,2},{261,18},{262,3},{263,19... | collective-permute-start | bytes 196616 | tf_op jit(solution)/shard_map/ppermute | solution.py:54
  3.9 0.7 collective-permute-start.2
  4.6 0.7 collective-permute-start.1
  5.2 0.7 collective-permute-start
  5.9 7.6 %all-to-all-start = ((f32[16,128,128]{2,1,0:T(8,128)}), f32[16,128,128]{2,1,0:T(8,128)S(1)}, u32[]{:S(2)}, u32[]{:S(2)}) async-start(f32[16,128,128]{2,1,0:T(8,128)} %broadcast_in_dim.9), calls=%async_computation | async-start | bytes 2097152 | tf_op jit(solution)/shard_map/all_to_all | solution.py:283
  13.5 8.2 %collective-permute-done.3 = f32[128,128]{1,0:T(8,128)S(1)} collective-permute-done((f32[128,128]{1,0:T(8,128)S(1)}, f32[128,128]{1,0:T(8,128)S(1)}, u32[]{:S(2)}, u32[]{:S(2)}) %collective-permute-start.3) | collective-permute-done | bytes 65568 | tf_op jit(solution)/shard_map/ppermute | solution.py:54
  21.7 1.3 %collective-permute-start.4 = (f32[128,128]{1,0:T(8,128)S(1)}, f32[128,128]{1,0:T(8,128)S(1)}, u32[]{:S(2)}, u32[]{:S(2)}) collective-permute-start(f32[128,128]{1,0:T(8,128)S(1)} %add_add_fusion.1), channel_id=1, source_target_pairs={{0,64},{128,192},{256,320},{384,448},{1,65},{129,193},{257,321},{3... | collective-permute-start | bytes 196616 | tf_op jit(solution)/shard_map/ppermute | solution.py:76
  23.0 1.3 %collective-permute-done.4 = f32[128,128]{1,0:T(8,128)S(1)} collective-permute-done((f32[128,128]{1,0:T(8,128)S(1)}, f32[128,128]{1,0:T(8,128)S(1)}, u32[]{:S(2)}, u32[]{:S(2)}) %collective-permute-start.4) | collective-permute-done | bytes 65568 | tf_op jit(solution)/shard_map/ppermute | solution.py:76
  24.3 1.3 %collective-permute-start.5 = (f32[128,128]{1,0:T(8,128)S(1)}, f32[128,128]{1,0:T(8,128)S(1)}, u32[]{:S(2)}, u32[]{:S(2)}) collective-permute-start(f32[128,128]{1,0:T(8,128)S(1)} %add.33), channel_id=1, source_target_pairs={{0,32},{64,96},{128,160},{192,224},{256,288},{320,352},{384,416},{... | collective-permute-start | bytes 196616 | tf_op jit(solution)/shard_map/ppermute | solution.py:76
  25.6 1.7 %collective-permute-done.5 = f32[128,128]{1,0:T(8,128)S(1)} collective-permute-done((f32[128,128]{1,0:T(8,128)S(1)}, f32[128,128]{1,0:T(8,128)S(1)}, u32[]{:S(2)}, u32[]{:S(2)}) %collective-permute-start.5) | collective-permute-done | bytes 65568 | tf_op jit(solution)/shard_map/ppermute | solution.py:76
  27.3 5.7 %collective-permute-start.6 = (f32[128,128]{1,0:T(8,128)S(1)}, f32[128,128]{1,0:T(8,128)S(1)}, u32[]{:S(2)}, u32[]{:S(2)}) collective-permute-start(f32[128,128]{1,0:T(8,128)S(1)} %add.34.mine), channel_id=1, source_target_pairs={{0,16},{16,0},{1,17},{17,1},{2,18},{18,2},{3,19},{19,3},{4,20},{20... | collective-permute-start | bytes 196616 | tf_op jit(solution)/shard_map/ppermute | solution.py:82
  33.1 0.9 collective-permute-done.6.other
  33.9 1.6 %copy-done = f32[2048,256]{1,0:T(8,128)S(1)} copy-done((f32[2048,256]{1,0:T(8,128)S(1)}, f32[2048,256]{1,0:T(8,128)}, u32[]{:S(2)}) %copy-start) | copy-done | bytes 2097176
  35.5 1.0 first.1.terms
  37.2 23.5 %all_to_all.20.terms = f32[16,136,128]{2,1,0:T(8,128)S(1)} all-to-all(f32[16,136,128]{2,1,0:T(8,128)S(1)} %cross.1), channel_id=1, replica_groups=mesh['z'=16,'core'=2,'y'=4,'x'=4] {'y','x'}, dimensions={0} | all-to-all | bytes 2228224 | tf_op jit(solution)/shard_map/all_to_all | solution.py:288
  60.9 3.7 %collective-permute-start.7 = (f32[8,128]{1,0:T(8,128)S(1)}, f32[8,128]{1,0:T(8,128)S(1)}, u32[]{:S(2)}, u32[]{:S(2)}) collective-permute-start(f32[8,128]{1,0:T(8,128)S(1)} %get-tuple-element.9.part), channel_id=1, source_target_pairs={{0,16},{16,0},{1,17},{17,1},{2,18},{18,2},{3,19},{19,3},{4,20},{20... | collective-permute-start | bytes 12296 | tf_op jit(solution)/shard_map/ppermute | solution.py:82
  64.6 1.3 %collective-permute-start.10 = (f32[128,128]{1,0:T(8,128)S(1)}, f32[128,128]{1,0:T(8,128)S(1)}, u32[]{:S(2)}, u32[]{:S(2)}) collective-permute-start(f32[128,128]{1,0:T(8,128)S(1)} %get-tuple-element.8.wmat), channel_id=1, source_target_pairs={{256,0},{257,16},{258,1},{259,17},{260,2},{261,18},{262,3},{263,19... | collective-permute-start | bytes 196616 | tf_op jit(solution)/shard_map/ppermute | solution.py:54
  65.9 0.7 collective-permute-start.9
  66.6 0.7 collective-permute-start.8
  67.9 16.9 %all-to-all-start.2 = ((f32[16,8,128]{2,1,0:T(8,128)}), f32[16,8,128]{2,1,0:T(8,128)S(1)}, u32[]{:S(2)}, u32[]{:S(2)}) async-start(f32[16,8,128]{2,1,0:T(8,128)} %spread.1), calls=%async_computation.2 | async-start | bytes 131072 | tf_op jit(solution)/shard_map/all_to_all | solution.py:292
  85.6 3.4 %all-to-all-done.2 = f32[16,8,128]{2,1,0:T(8,128)S(1)} async-done(((f32[16,8,128]{2,1,0:T(8,128)}), f32[16,8,128]{2,1,0:T(8,128)S(1)}, u32[]{:S(2)}, u32[]{:S(2)}) %all-to-all-start.2) | async-done | bytes 65568 | tf_op jit(solution)/shard_map/all_to_all | solution.py:292
  89.0 1.1 broadcast_in_dim.11
  90.1 4.0 %all-to-all-start.3 = ((f32[16,136,128]{2,1,0:T(8,128)}), f32[16,136,128]{2,1,0:T(8,128)S(1)}, u32[]{:S(2)}, u32[]{:S(2)}) async-start(f32[16,136,128]{2,1,0:T(8,128)} %broadcast_in_dim.11), calls=%async_computation.3 | async-start | bytes 2228224 | tf_op jit(solution)/shard_map/all_to_all | solution.py:44
  94.1 3.2 %collective-permute-start.12 = (f32[128,128]{1,0:T(8,128)S(1)}, f32[128,128]{1,0:T(8,128)S(1)}, u32[]{:S(2)}, u32[]{:S(2)}) collective-permute-start(f32[128,128]{1,0:T(8,128)S(1)} %add.37), channel_id=1, source_target_pairs={{0,64},{128,192},{256,320},{384,448},{1,65},{129,193},{257,321},{3... | collective-permute-start | bytes 196616 | tf_op jit(solution)/shard_map/ppermute | solution.py:76
  97.3 1.3 %collective-permute-done.12 = f32[128,128]{1,0:T(8,128)S(1)} collective-permute-done((f32[128,128]{1,0:T(8,128)S(1)}, f32[128,128]{1,0:T(8,128)S(1)}, u32[]{:S(2)}, u32[]{:S(2)}) %collective-permute-start.12) | collective-permute-done | bytes 65568 | tf_op jit(solution)/shard_map/ppermute | solution.py:76
  98.6 1.3 %collective-permute-start.13 = (f32[128,128]{1,0:T(8,128)S(1)}, f32[128,128]{1,0:T(8,128)S(1)}, u32[]{:S(2)}, u32[]{:S(2)}) collective-permute-start(f32[128,128]{1,0:T(8,128)S(1)} %add.38), channel_id=1, source_target_pairs={{0,32},{64,96},{128,160},{192,224},{256,288},{320,352},{384,416},{... | collective-permute-start | bytes 196616 | tf_op jit(solution)/shard_map/ppermute | solution.py:76
  99.9 1.6 %collective-permute-done.13 = f32[128,128]{1,0:T(8,128)S(1)} collective-permute-done((f32[128,128]{1,0:T(8,128)S(1)}, f32[128,128]{1,0:T(8,128)S(1)}, u32[]{:S(2)}, u32[]{:S(2)}) %collective-permute-start.13) | collective-permute-done | bytes 65568 | tf_op jit(solution)/shard_map/ppermute | solution.py:76
  101.6 5.2 %collective-permute-start.14 = (f32[128,128]{1,0:T(8,128)S(1)}, f32[128,128]{1,0:T(8,128)S(1)}, u32[]{:S(2)}, u32[]{:S(2)}) collective-permute-start(f32[128,128]{1,0:T(8,128)S(1)} %add.39.wmine), channel_id=1, source_target_pairs={{0,16},{16,0},{1,17},{17,1},{2,18},{18,2},{3,19},{19,3},{4,20},{20... | collective-permute-start | bytes 196616 | tf_op jit(solution)/shard_map/ppermute | solution.py:82
  106.8 0.9 collective-permute-done.14.wother
  107.7 2.9 %all-to-all-done.3.found = f32[16,136,128]{2,1,0:T(8,128)S(1)} async-done(((f32[16,136,128]{2,1,0:T(8,128)}), f32[16,136,128]{2,1,0:T(8,128)S(1)}, u32[]{:S(2)}, u32[]{:S(2)}) %all-to-all-start.3) | async-done | bytes 1114144 | tf_op jit(solution)/shard_map/all_to_all | solution.py:44
  110.6 4.6 %last.1 = (f32[2048,256]{1,0:T(8,128)}, f32[128,128]{1,0:T(8,128)}) custom-call(f32[2048,256]{1,0:T(8,128)} %slab.3, f32[16,128,128]{2,1,0:T(8,128)S(1)} %all-to-all-done.rows, f32[16,136,128]{2,1,0:T(8,128)S(1)} %all-to-all-done.3.found, f32[128,128]{1,0:T(8,128)S(1)} %copy-done.1, f32[128,128]{1,0:T(8,128)S(1)} %get-tuple-element.8.wmat, ...), custom_call_target="tpu_custom_call" | custom-call | flops 805306368 | bytes 6291456 | tf_op jit(solution)/shard_map/last/pallas_call | solution.py:259
  (31 shorter events, 2.3 us)
Async XLA Ops:
  0.6 2.0 %copy-start.1 = (f32[128,128]{1,0:T(8,128)S(1)}, f32[128,128]{1,0:T(8,128)}, u32[]{:S(2)}) copy-start(f32[128,128]{1,0:T(8,128)} %panel.3) | copy-start | bytes 196612
  2.6 19.1 %collective-permute-start.3 = (f32[128,128]{1,0:T(8,128)S(1)}, f32[128,128]{1,0:T(8,128)S(1)}, u32[]{:S(2)}, u32[]{:S(2)}) collective-permute-start(f32[128,128]{1,0:T(8,128)S(1)} %copy-done.1), channel_id=1, source_target_pairs={{256,0},{257,16},{258,1},{259,17},{260,2},{261,18},{262,3},{263,19... | collective-permute-start | bytes 196616 | tf_op jit(solution)/shard_map/ppermute | solution.py:54
  3.9 17.8 %collective-permute-start.2 = (f32[128,128]{1,0:T(8,128)S(1)}, f32[128,128]{1,0:T(8,128)S(1)}, u32[]{:S(2)}, u32[]{:S(2)}) collective-permute-start(f32[128,128]{1,0:T(8,128)S(1)} %copy-done.1), channel_id=1, source_target_pairs={{256,128},{257,144},{258,129},{259,145},{260,130},{261,146},{262,1... | collective-permute-start | bytes 196616 | tf_op jit(solution)/shard_map/ppermute | solution.py:54
  4.6 17.1 %collective-permute-start.1 = (f32[128,128]{1,0:T(8,128)S(1)}, f32[128,128]{1,0:T(8,128)S(1)}, u32[]{:S(2)}, u32[]{:S(2)}) collective-permute-start(f32[128,128]{1,0:T(8,128)S(1)} %copy-done.1), channel_id=1, source_target_pairs={{256,256},{257,272},{258,257},{259,273},{260,258},{261,274},{262,2... | collective-permute-start | bytes 196616 | tf_op jit(solution)/shard_map/ppermute | solution.py:54
  5.2 16.4 %collective-permute-start = (f32[128,128]{1,0:T(8,128)S(1)}, f32[128,128]{1,0:T(8,128)S(1)}, u32[]{:S(2)}, u32[]{:S(2)}) collective-permute-start(f32[128,128]{1,0:T(8,128)S(1)} %copy-done.1), channel_id=1, source_target_pairs={{256,384},{257,400},{258,385},{259,401},{260,386},{261,402},{262,3... | collective-permute-start | bytes 196616 | tf_op jit(solution)/shard_map/ppermute | solution.py:54
  5.9 30.6 %all-to-all-start = ((f32[16,128,128]{2,1,0:T(8,128)}), f32[16,128,128]{2,1,0:T(8,128)S(1)}, u32[]{:S(2)}, u32[]{:S(2)}) async-start(f32[16,128,128]{2,1,0:T(8,128)} %broadcast_in_dim.9), calls=%async_computation | async-start | bytes 2097152 | tf_op jit(solution)/shard_map/all_to_all | solution.py:283
  21.7 2.6 %collective-permute-start.4 = (f32[128,128]{1,0:T(8,128)S(1)}, f32[128,128]{1,0:T(8,128)S(1)}, u32[]{:S(2)}, u32[]{:S(2)}) collective-permute-start(f32[128,128]{1,0:T(8,128)S(1)} %add_add_fusion.1), channel_id=1, source_target_pairs={{0,64},{128,192},{256,320},{384,448},{1,65},{129,193},{257,321},{3... | collective-permute-start | bytes 196616 | tf_op jit(solution)/shard_map/ppermute | solution.py:76
  24.3 3.0 %collective-permute-start.5 = (f32[128,128]{1,0:T(8,128)S(1)}, f32[128,128]{1,0:T(8,128)S(1)}, u32[]{:S(2)}, u32[]{:S(2)}) collective-permute-start(f32[128,128]{1,0:T(8,128)S(1)} %add.33), channel_id=1, source_target_pairs={{0,32},{64,96},{128,160},{192,224},{256,288},{320,352},{384,416},{... | collective-permute-start | bytes 196616 | tf_op jit(solution)/shard_map/ppermute | solution.py:76
  27.3 6.6 %collective-permute-start.6 = (f32[128,128]{1,0:T(8,128)S(1)}, f32[128,128]{1,0:T(8,128)S(1)}, u32[]{:S(2)}, u32[]{:S(2)}) collective-permute-start(f32[128,128]{1,0:T(8,128)S(1)} %add.34.mine), channel_id=1, source_target_pairs={{0,16},{16,0},{1,17},{17,1},{2,18},{18,2},{3,19},{19,3},{4,20},{20... | collective-permute-start | bytes 196616 | tf_op jit(solution)/shard_map/ppermute | solution.py:82
  33.9 1.6 %copy-start = (f32[2048,256]{1,0:T(8,128)S(1)}, f32[2048,256]{1,0:T(8,128)}, u32[]{:S(2)}) copy-start(f32[2048,256]{1,0:T(8,128)} %slab.3) | copy-start | bytes 6291460
  35.5 1.0 copy-start.3
  37.2 23.5 %copy-start.2 = (f32[128,128]{1,0:T(8,128)S(1)}, f32[128,128]{1,0:T(8,128)}, u32[]{:S(2)}) copy-start(f32[128,128]{1,0:T(8,128)} %tfactor.3) | copy-start | bytes 196612
  60.9 6.3 %collective-permute-start.7 = (f32[8,128]{1,0:T(8,128)S(1)}, f32[8,128]{1,0:T(8,128)S(1)}, u32[]{:S(2)}, u32[]{:S(2)}) collective-permute-start(f32[8,128]{1,0:T(8,128)S(1)} %get-tuple-element.9.part), channel_id=1, source_target_pairs={{0,16},{16,0},{1,17},{17,1},{2,18},{18,2},{3,19},{19,3},{4,20},{20... | collective-permute-start | bytes 12296 | tf_op jit(solution)/shard_map/ppermute | solution.py:82
  64.6 20.9 %collective-permute-start.10 = (f32[128,128]{1,0:T(8,128)S(1)}, f32[128,128]{1,0:T(8,128)S(1)}, u32[]{:S(2)}, u32[]{:S(2)}) collective-permute-start(f32[128,128]{1,0:T(8,128)S(1)} %get-tuple-element.8.wmat), channel_id=1, source_target_pairs={{256,0},{257,16},{258,1},{259,17},{260,2},{261,18},{262,3},{263,19... | collective-permute-start | bytes 196616 | tf_op jit(solution)/shard_map/ppermute | solution.py:54
  65.9 19.6 %collective-permute-start.9 = (f32[128,128]{1,0:T(8,128)S(1)}, f32[128,128]{1,0:T(8,128)S(1)}, u32[]{:S(2)}, u32[]{:S(2)}) collective-permute-start(f32[128,128]{1,0:T(8,128)S(1)} %get-tuple-element.8.wmat), channel_id=1, source_target_pairs={{256,128},{257,144},{258,129},{259,145},{260,130},{261,146},{262,1... | collective-permute-start | bytes 196616 | tf_op jit(solution)/shard_map/ppermute | solution.py:54
  66.6 18.9 %collective-permute-start.8 = (f32[128,128]{1,0:T(8,128)S(1)}, f32[128,128]{1,0:T(8,128)S(1)}, u32[]{:S(2)}, u32[]{:S(2)}) collective-permute-start(f32[128,128]{1,0:T(8,128)S(1)} %get-tuple-element.8.wmat), channel_id=1, source_target_pairs={{256,384},{257,400},{258,385},{259,401},{260,386},{261,402},{262,3... | collective-permute-start | bytes 196616 | tf_op jit(solution)/shard_map/ppermute | solution.py:54
  67.9 21.1 %all-to-all-start.2 = ((f32[16,8,128]{2,1,0:T(8,128)}), f32[16,8,128]{2,1,0:T(8,128)S(1)}, u32[]{:S(2)}, u32[]{:S(2)}) async-start(f32[16,8,128]{2,1,0:T(8,128)} %spread.1), calls=%async_computation.2 | async-start | bytes 131072 | tf_op jit(solution)/shard_map/all_to_all | solution.py:292
  84.8 9.3 %collective-permute-start.11 = (f32[128,128]{1,0:T(8,128)S(1)}, f32[128,128]{1,0:T(8,128)S(1)}, u32[]{:S(2)}, u32[]{:S(2)}) collective-permute-start(f32[128,128]{1,0:T(8,128)S(1)} %get-tuple-element.8.wmat), channel_id=1, source_target_pairs={{256,256},{257,272},{258,257},{259,273},{260,258},{261,274},{262,2... | collective-permute-start | bytes 196616 | tf_op jit(solution)/shard_map/ppermute | solution.py:54
  90.1 20.5 %all-to-all-start.3 = ((f32[16,136,128]{2,1,0:T(8,128)}), f32[16,136,128]{2,1,0:T(8,128)S(1)}, u32[]{:S(2)}, u32[]{:S(2)}) async-start(f32[16,136,128]{2,1,0:T(8,128)} %broadcast_in_dim.11), calls=%async_computation.3 | async-start | bytes 2228224 | tf_op jit(solution)/shard_map/all_to_all | solution.py:44
  94.1 4.5 %collective-permute-start.12 = (f32[128,128]{1,0:T(8,128)S(1)}, f32[128,128]{1,0:T(8,128)S(1)}, u32[]{:S(2)}, u32[]{:S(2)}) collective-permute-start(f32[128,128]{1,0:T(8,128)S(1)} %add.37), channel_id=1, source_target_pairs={{0,64},{128,192},{256,320},{384,448},{1,65},{129,193},{257,321},{3... | collective-permute-start | bytes 196616 | tf_op jit(solution)/shard_map/ppermute | solution.py:76
  98.6 2.9 %collective-permute-start.13 = (f32[128,128]{1,0:T(8,128)S(1)}, f32[128,128]{1,0:T(8,128)S(1)}, u32[]{:S(2)}, u32[]{:S(2)}) collective-permute-start(f32[128,128]{1,0:T(8,128)S(1)} %add.38), channel_id=1, source_target_pairs={{0,32},{64,96},{128,160},{192,224},{256,288},{320,352},{384,416},{... | collective-permute-start | bytes 196616 | tf_op jit(solution)/shard_map/ppermute | solution.py:76
  101.6 6.1 %collective-permute-start.14 = (f32[128,128]{1,0:T(8,128)S(1)}, f32[128,128]{1,0:T(8,128)S(1)}, u32[]{:S(2)}, u32[]{:S(2)}) collective-permute-start(f32[128,128]{1,0:T(8,128)S(1)} %add.39.wmine), channel_id=1, source_target_pairs={{0,16},{16,0},{1,17},{17,1},{2,18},{18,2},{3,19},{19,3},{4,20},{20... | collective-permute-start | bytes 196616 | tf_op jit(solution)/shard_map/ppermute | solution.py:82
